TPU v7x, 256 devices: a whole 4x4x8 slice. The times are simulated.
256 devices in a mesh: gx: 32 (over x, y, core), gy: 8 (over z).
Axes of the slice: x: 4, y: 4, z: 8, core: 2. Of those that a mesh axis runs over, the one named last changes fastest.
Arguments:
- fine_field: bfloat16 [64, 128, 64, 128], P('gx', 'gy'), may hold values from -6 to 6
- down_weight: bfloat16 [8, 128, 256], replicated, may hold values from -0.1875 to 0.1875
- conv_weight: bfloat16 [27, 256, 256], replicated, may hold values from -0.078125 to 0.078125
- coarse_cotangent: bfloat16 [32, 64, 32, 256], P('gx', 'gy'), may hold values from -6 to 6
Outputs:
- fine_grad: bfloat16 [64, 128, 64, 128], P('gx', 'gy')
- conv_weight_grad: bfloat16 [27, 256, 256], replicated
- down_weight_grad: bfloat16 [8, 128, 256], replicated
All inputs are finite; a program needn't handle non-finite values.
Results may differ from a plain program's by a relative error of at most 0.0065.
Values may be sent and summed in bfloat16 or wider, within the bound.
A program may use at most 64 MiB of HBM per device.

v0:
```python
import jax
import jax.numpy as jnp
from jax import lax
from jax.sharding import PartitionSpec as P


def padded_2(x, sides, width):
    for axis, dim in sides:
        peers, length = (lax.axis_size(axis), x.shape[dim])
        up = [(i, (i + 1) % peers) for i in range(peers - 1)]
        down = [(j, i) for i, j in up]
        last = lax.slice_in_dim(x, length - width, length, axis=dim)
        first = lax.slice_in_dim(x, 0, width, axis=dim)
        before = lax.ppermute(last, axis, up)
        after = lax.ppermute(first, axis, down)
        x = jnp.concatenate([before, x, after], axis=dim)
    return x


def to_blocks(field, count_x, count_y, count_z, width):
    shaped = field.reshape(count_x, 2, count_y, 2, count_z, 2, width)
    return shaped.transpose(0, 2, 4, 1, 3, 5, 6).reshape(count_x * count_y * count_z, 8 * width)


def from_blocks(blocks, count_x, count_y, count_z, width):
    shaped = blocks.reshape(count_x, count_y, count_z, 2, 2, 2, width)
    return shaped.transpose(0, 3, 1, 4, 2, 5, 6).reshape(
        2 * count_x, 2 * count_y, 2 * count_z, width
    )


def extend(field):
    widened = padded_2(field, (("gx", 0), ("gy", 1)), 1)
    return jnp.pad(widened, ((0, 0), (0, 0), (1, 1), (0, 0)))


def gather_taps(padded, count_x, count_y, count_z, width, mirror):
    pieces = []
    for first in range(3):
        for second in range(3):
            for third in range(3):
                if mirror:
                    lower = (2 - first, 2 - second, 2 - third)
                else:
                    lower = (first, second, third)
                pieces.append(
                    padded[
                        lower[0] : lower[0] + count_x,
                        lower[1] : lower[1] + count_y,
                        lower[2] : lower[2] + count_z,
                    ]
                )
    stacked = jnp.stack(pieces, axis=3)
    return stacked.reshape(count_x * count_y * count_z, 27 * width)


def on_device(fine_field, down_weight, conv_weight, coarse_cotangent):
    count_x, count_y, count_z, width = coarse_cotangent.shape
    narrow = fine_field.shape[3]
    blocks = to_blocks(fine_field, count_x, count_y, count_z, narrow)
    down_flat = down_weight.reshape(8 * narrow, width)
    hidden = jnp.dot(blocks, down_flat, preferred_element_type=jnp.float32).astype(jnp.bfloat16)
    patches = gather_taps(
        extend(hidden.reshape(count_x, count_y, count_z, width)),
        count_x,
        count_y,
        count_z,
        width,
        False,
    )
    preact = jnp.dot(
        patches, conv_weight.reshape(27 * width, width), preferred_element_type=jnp.float32
    )
    sig = jax.nn.sigmoid(preact)
    cotangent = coarse_cotangent.reshape(-1, width).astype(jnp.float32)
    pre_grad = (cotangent * (sig * (1.0 + preact * (1.0 - sig)))).astype(jnp.bfloat16)
    conv_local = lax.dot_general(
        patches, pre_grad, (((0,), (0,)), ((), ())), preferred_element_type=jnp.float32
    )
    grad_patches = gather_taps(
        extend(pre_grad.reshape(count_x, count_y, count_z, width)),
        count_x,
        count_y,
        count_z,
        width,
        True,
    )
    turned = conv_weight.transpose(0, 2, 1).reshape(27 * width, width)
    back = jnp.dot(grad_patches, turned, preferred_element_type=jnp.float32)
    hidden_grad = (cotangent + back).astype(jnp.bfloat16)
    fine_flat = lax.dot_general(
        hidden_grad, down_flat, (((1,), (1,)), ((), ())), preferred_element_type=jnp.float32
    ).astype(jnp.bfloat16)
    fine_grad = from_blocks(fine_flat, count_x, count_y, count_z, narrow)
    down_local = lax.dot_general(
        blocks, hidden_grad, (((0,), (0,)), ((), ())), preferred_element_type=jnp.float32
    )
    conv_flat = conv_local.reshape(-1)
    down_vector = down_local.reshape(-1)
    conv_total, down_total = lax.psum((conv_flat, down_vector), ("gx", "gy"))
    conv_rounded = conv_total.astype(jnp.bfloat16)
    down_rounded = down_total.astype(jnp.bfloat16)
    conv_weight_grad = conv_rounded.reshape(27, width, width)
    down_weight_grad = down_rounded.reshape(8, narrow, width)
    return (fine_grad, conv_weight_grad, down_weight_grad)


def solution(mesh):
    in_specs = (P("gx", "gy", None, None), P(), P(), P("gx", "gy", None, None))
    out_specs = (P("gx", "gy", None, None), P(), P())
    return jax.shard_map(
        on_device, mesh=mesh, in_specs=in_specs, out_specs=out_specs, check_vma=False
    )
```

profile of v0, /device:TPU:1, one launch (start us, length us, event | category | flops | bytes accessed | tf_op | source)
XLA Modules:
  0.0 232.2 jit_solution(12564009155630655214)
XLA Ops:
  0.6 0.0 copy-start
  0.6 1.5 copy.75
  2.1 0.4 reshape.57
  2.5 0.0 copy-done
  2.5 0.3 convolution_convert_fusion.1
  2.8 5.1 %collective-permute-start.1 = (bf16[1,8,32,256]{3,2,1,0:T(8,128)(2,1)S(1)}, bf16[1,8,32,256]{3,2,1,0:T(8,128)(2,1)S(1)}, u32[]{:S(2)}, u32[]{:S(2)}) collective-permute-start(bf16[1,8,32,256]{3,2,1,0:T(8,128)(2,1)S(1)} %bitcast.249), channel_id=1, source_target_pairs={{8,0},{16,8},{24,16},{32,24},{40,32},{48,40},{56,48},{64,56},{72,6... | collective-permute-start | bytes 393224 | tf_op jit(solution)/shard_map/ppermute | solution.py:15
  8.0 1.9 collective-permute-start
  9.9 0.2 collective-permute-done.1
  10.0 1.8 collective-permute-done
  11.8 3.0 %collective-permute-start.2 = (bf16[3,1,32,256]{3,2,1,0:T(8,128)(2,1)S(1)}, bf16[3,1,32,256]{3,2,1,0:T(8,128)(2,1)S(1)}, u32[]{:S(2)}, u32[]{:S(2)}) collective-permute-start(bf16[3,1,32,256]{3,2,1,0:T(8,128)(2,1)S(1)} %get-tuple-element.7), channel_id=1, source_target_pairs={{0,1},{1,2},{2,3},{3,4},{4,5},{5,6},{6,7},{8,9},{9,10},{10,11},{11... | collective-permute-start | bytes 147464 | tf_op jit(solution)/shard_map/ppermute | solution.py:14
  14.8 1.3 collective-permute-start.3
  16.1 0.0 collective-permute-done.2
  16.1 3.7 %collective-permute-done.3 = bf16[3,1,32,256]{3,2,1,0:T(8,128)(2,1)S(1)} collective-permute-done((bf16[3,1,32,256]{3,2,1,0:T(8,128)(2,1)S(1)}, bf16[3,1,32,256]{3,2,1,0:T(8,128)(2,1)S(1)}, u32[]{:S(2)}, u32[]{:S(2)}) %collective-permute-start.3) | collective-permute-done | bytes 49184 | tf_op jit(solution)/shard_map/ppermute | solution.py:15
  19.8 0.3 fusion.11
  20.9 2.3 copy.65
  23.2 0.0 copy-start.2
  23.3 0.0 copy-start.4
  23.3 3.7 %copy.70 = bf16[32,8,27,256]{3,1,2,0:T(8,128)(2,1)S(1)} copy(bf16[32,8,27,256]{3,2,1,0:T(8,128)(2,1)S(1)} %bitcast.245) | data formatting | bytes 7077888
  27.0 0.0 copy-start.1
  27.0 0.0 copy-done.2
  27.0 0.0 copy-done.4
  27.0 1.1 fusion.16
  28.1 0.7 copy-done.1
  28.8 1.9 collective-permute-start.5
  30.7 5.6 %collective-permute-start.4 = (bf16[1,8,32,256]{3,2,1,0:T(8,128)(2,1)S(1)}, bf16[1,8,32,256]{3,2,1,0:T(8,128)(2,1)S(1)}, u32[]{:S(2)}, u32[]{:S(2)}) collective-permute-start(bf16[1,8,32,256]{3,2,1,0:T(8,128)(2,1)S(1)} %bitcast.261), channel_id=1, source_target_pairs={{0,8},{8,16},{16,24},{24,32},{32,40},{40,48},{48,56},{56,64},{64,7... | collective-permute-start | bytes 393224 | tf_op jit(solution)/shard_map/ppermute | solution.py:14
  36.3 5.7 %copy.67 = bf16[27,256,256]{1,2,0:T(8,128)(2,1)} copy(bf16[27,256,256]{2,1,0:T(8,128)(2,1)} %param.6) | data formatting | bytes 7077888 | tf_op args[2]
  42.1 0.0 collective-permute-done.5
  42.1 0.0 collective-permute-done.4
  42.1 3.5 %collective-permute-start.6 = (bf16[3,1,32,256]{3,2,1,0:T(8,128)(2,1)S(1)}, bf16[3,1,32,256]{3,2,1,0:T(8,128)(2,1)S(1)}, u32[]{:S(2)}, u32[]{:S(2)}) collective-permute-start(bf16[3,1,32,256]{3,2,1,0:T(8,128)(2,1)S(1)} %get-tuple-element.5), channel_id=1, source_target_pairs={{0,1},{1,2},{2,3},{3,4},{4,5},{5,6},{6,7},{8,9},{9,10},{10,11},{11... | collective-permute-start | bytes 147464 | tf_op jit(solution)/shard_map/ppermute | solution.py:14
  45.6 1.5 collective-permute-start.7
  47.1 6.1 %convolution_bitcast_fusion = f32[864,2,8,128]{3,2,1,0:T(8,128)} fusion(bf16[256,6912]{1,0:T(8,128)(2,1)} %bitcast.248, bf16[256,256]{1,0:T(8,128)(2,1)S(1)} %bitcast.280, f32[256,256]{1,0:T(8,128)S(1)} %get-tuple-element.10), kind=kOutput, calls=%fused_computation | convolution fusion | flops 906625024 | bytes 11010048 | tf_op jit(solution)/shard_map/dot_general | solution.py:77
  53.2 9.6 %copy.72 = f32[864,2,8,128]{3,1,2,0:T(2,128)} copy(f32[864,2,8,128]{3,2,1,0:T(8,128)} %convolution_bitcast_fusion) | data formatting | bytes 14155776
  62.8 0.0 collective-permute-done.6
  62.8 0.0 collective-permute-done.7
  62.8 0.3 select_maximum_fusion
  63.9 2.3 copy.66
  66.2 0.0 copy-start.3
  66.2 3.9 %copy.71 = bf16[32,8,27,256]{3,1,2,0:T(8,128)(2,1)S(1)} copy(bf16[32,8,27,256]{3,2,1,0:T(8,128)(2,1)S(1)} %bitcast.246) | data formatting | bytes 7077888
  70.1 0.0 copy-done.3
  70.1 1.1 fusion.1
  71.2 0.3 convolution_bitcast_fusion.1
  71.5 0.3 convolution_convert_fusion
  71.9 0.3 copy.69
  72.2 0.5 copy.73
  72.7 150.3 %all-reduce.4 = (bf16[1769472]{0:T(1024)(128)(2,1)}, bf16[262144]{0:T(1024)(128)(2,1)S(1)}) all-reduce(f32[1769472]{0:T(1024)} %bitcast.244, f32[262144]{0:T(1024)S(1)} %bitcast.272), channel_id=1, replica_groups=mesh['gx'=32,'gy'=8] {'gx','gy'}, use_global_device_ids=true, to_apply=%region_0.1 | all-reduce | flops 2031616 | bytes 12189696 | tf_op jit(solution)/shard_map/psum | solution.py:100
  223.1 6.4 %reshape.68 = bf16[27,256,256]{2,1,0:T(8,128)(2,1)} reshape(bf16[1769472]{0:T(1024)(128)(2,1)} %get-tuple-element.3) | data formatting | bytes 7077888 | tf_op jit(solution)/shard_map/reshape | solution.py:103
  229.5 0.4 reshape.65
  229.8 1.4 copy.68
  231.2 1.0 reshape.70
  (56 shorter events, 1.1 us)
Async XLA Ops:
  0.6 1.9 copy-start
  2.8 7.2 %collective-permute-start.1 = (bf16[1,8,32,256]{3,2,1,0:T(8,128)(2,1)S(1)}, bf16[1,8,32,256]{3,2,1,0:T(8,128)(2,1)S(1)}, u32[]{:S(2)}, u32[]{:S(2)}) collective-permute-start(bf16[1,8,32,256]{3,2,1,0:T(8,128)(2,1)S(1)} %bitcast.249), channel_id=1, source_target_pairs={{8,0},{16,8},{24,16},{32,24},{40,32},{48,40},{56,48},{64,56},{72,6... | collective-permute-start | bytes 393224 | tf_op jit(solution)/shard_map/ppermute | solution.py:15
  8.0 3.9 %collective-permute-start = (bf16[1,8,32,256]{3,2,1,0:T(8,128)(2,1)S(1)}, bf16[1,8,32,256]{3,2,1,0:T(8,128)(2,1)S(1)}, u32[]{:S(2)}, u32[]{:S(2)}) collective-permute-start(bf16[1,8,32,256]{3,2,1,0:T(8,128)(2,1)S(1)} %bitcast.250), channel_id=1, source_target_pairs={{0,8},{8,16},{16,24},{24,32},{32,40},{40,48},{48,56},{56,64},{64,7... | collective-permute-start | bytes 393224 | tf_op jit(solution)/shard_map/ppermute | solution.py:14
  11.8 4.3 %collective-permute-start.2 = (bf16[3,1,32,256]{3,2,1,0:T(8,128)(2,1)S(1)}, bf16[3,1,32,256]{3,2,1,0:T(8,128)(2,1)S(1)}, u32[]{:S(2)}, u32[]{:S(2)}) collective-permute-start(bf16[3,1,32,256]{3,2,1,0:T(8,128)(2,1)S(1)} %get-tuple-element.7), channel_id=1, source_target_pairs={{0,1},{1,2},{2,3},{3,4},{4,5},{5,6},{6,7},{8,9},{9,10},{10,11},{11... | collective-permute-start | bytes 147464 | tf_op jit(solution)/shard_map/ppermute | solution.py:14
  14.8 5.0 %collective-permute-start.3 = (bf16[3,1,32,256]{3,2,1,0:T(8,128)(2,1)S(1)}, bf16[3,1,32,256]{3,2,1,0:T(8,128)(2,1)S(1)}, u32[]{:S(2)}, u32[]{:S(2)}) collective-permute-start(bf16[3,1,32,256]{3,2,1,0:T(8,128)(2,1)S(1)} %get-tuple-element.8), channel_id=1, source_target_pairs={{1,0},{2,1},{3,2},{4,3},{5,4},{6,5},{7,6},{9,8},{10,9},{11,10},{12... | collective-permute-start | bytes 147464 | tf_op jit(solution)/shard_map/ppermute | solution.py:15
  23.2 3.7 %copy-start.2 = (bf16[27,256,256]{2,1,0:T(8,128)(2,1)S(1)}, bf16[27,256,256]{2,1,0:T(8,128)(2,1)}, u32[]{:S(2)}) copy-start(bf16[27,256,256]{2,1,0:T(8,128)(2,1)} %param.6) | copy-start | bytes 10616836
  23.3 3.7 %copy-start.4 = (bf16[1,8,32,256]{3,2,1,0:T(8,128)(2,1)S(1)}, bf16[1,8,32,256]{3,2,1,0:T(8,128)(2,1)}, u32[]{:S(2)}) copy-start(bf16[1,8,32,256]{3,2,1,0:T(8,128)(2,1)} %param.7) | copy-start | bytes 393220
  27.0 1.9 copy-start.1
  28.8 13.2 %collective-permute-start.5 = (bf16[1,8,32,256]{3,2,1,0:T(8,128)(2,1)S(1)}, bf16[1,8,32,256]{3,2,1,0:T(8,128)(2,1)S(1)}, u32[]{:S(2)}, u32[]{:S(2)}) collective-permute-start(bf16[1,8,32,256]{3,2,1,0:T(8,128)(2,1)S(1)} %bitcast.260), channel_id=1, source_target_pairs={{8,0},{16,8},{24,16},{32,24},{40,32},{48,40},{56,48},{64,56},{72,6... | collective-permute-start | bytes 393224 | tf_op jit(solution)/shard_map/ppermute | solution.py:15
  30.7 11.3 %collective-permute-start.4 = (bf16[1,8,32,256]{3,2,1,0:T(8,128)(2,1)S(1)}, bf16[1,8,32,256]{3,2,1,0:T(8,128)(2,1)S(1)}, u32[]{:S(2)}, u32[]{:S(2)}) collective-permute-start(bf16[1,8,32,256]{3,2,1,0:T(8,128)(2,1)S(1)} %bitcast.261), channel_id=1, source_target_pairs={{0,8},{8,16},{16,24},{24,32},{32,40},{40,48},{48,56},{56,64},{64,7... | collective-permute-start | bytes 393224 | tf_op jit(solution)/shard_map/ppermute | solution.py:14
  42.1 20.7 %collective-permute-start.6 = (bf16[3,1,32,256]{3,2,1,0:T(8,128)(2,1)S(1)}, bf16[3,1,32,256]{3,2,1,0:T(8,128)(2,1)S(1)}, u32[]{:S(2)}, u32[]{:S(2)}) collective-permute-start(bf16[3,1,32,256]{3,2,1,0:T(8,128)(2,1)S(1)} %get-tuple-element.5), channel_id=1, source_target_pairs={{0,1},{1,2},{2,3},{3,4},{4,5},{5,6},{6,7},{8,9},{9,10},{10,11},{11... | collective-permute-start | bytes 147464 | tf_op jit(solution)/shard_map/ppermute | solution.py:14
  45.6 17.1 %collective-permute-start.7 = (bf16[3,1,32,256]{3,2,1,0:T(8,128)(2,1)S(1)}, bf16[3,1,32,256]{3,2,1,0:T(8,128)(2,1)S(1)}, u32[]{:S(2)}, u32[]{:S(2)}) collective-permute-start(bf16[3,1,32,256]{3,2,1,0:T(8,128)(2,1)S(1)} %get-tuple-element.6), channel_id=1, source_target_pairs={{1,0},{2,1},{3,2},{4,3},{5,4},{6,5},{7,6},{9,8},{10,9},{11,10},{12... | collective-permute-start | bytes 147464 | tf_op jit(solution)/shard_map/ppermute | solution.py:15
  66.2 3.9 %copy-start.3 = (bf16[27,256,256]{1,2,0:T(8,128)(2,1)S(1)}, bf16[27,256,256]{1,2,0:T(8,128)(2,1)}, u32[]{:S(2)}) copy-start(bf16[27,256,256]{1,2,0:T(8,128)(2,1)} %copy.67) | copy-start | bytes 10616836
where the time goes:
time: 233 us; the launch traced here: 232 us
  blocking collectives  150 us (64%)
  local copies, waits for them, and re-layouts  40.9 us (18%)
  starting transfers between devices  23.9 us (10%)
  matrix products  9.26 us (4%)
  waiting for transfers between devices  5.65 us (2%)
    psum x1, blocking collectives, on_device(): conv_total, down_total = lax.psum((conv_flat, down_vector), ('gx', 'gy'))  150 us
    unnamed x55, local copies, waits for them, and re-layouts  25 us
    ppermute x4, starting transfers between devices, padded_2(): before = lax.ppermute(last, axis, up)  14.1 us
    ppermute x4, starting transfers between devices, padded_2(): after = lax.ppermute(first, axis, down)  9.82 us
    reshape x1, local copies, waits for them, and re-layouts, on_device(): conv_weight_grad = conv_rounded.reshape(27, width, width)  6.4 us
    dot_general x1, matrix products, on_device(): lax.dot_general(patches, pre_grad, (((0,), (0,)), ((), ())), preferred_el...  6.09 us
    another operation x4, local copies, waits for them, and re-layouts, gather_taps(): stacked = jnp.stack(pieces, axis=3)  4.69 us
  transfers between devices with their start and end apart: 8, of which 3 were waited for; matrix products, arithmetic and copies ran while one was open for 9% of the time, Pallas kernels for 0%

commit v1 on v0

v1 whole, which is shorter than its diff:
```python
import jax
import jax.numpy as jnp
from jax import lax
from jax.experimental import pallas as pl
from jax.experimental.pallas import tpu as pltpu
from jax.sharding import PartitionSpec as P

MESH = pl.DeviceIdType.MESH
BF = jnp.bfloat16
F32 = jnp.float32

STREAMS = ((0, 7, True), (7, 7, False), (14, 7, True), (21, 6, False), (27, 4, True))
CONV_STREAMS = 4


def dot(a, b):
    return jnp.dot(a, b, preferred_element_type=F32)


def dot_t(a, b):
    return lax.dot_general(a, b, (((1,), (1,)), ((), ())), preferred_element_type=F32)


def iotas(n):
    return lax.broadcasted_iota(jnp.int32, (n, n), 0), lax.broadcasted_iota(jnp.int32, (n, n), 1)


def ones_where(mask):
    return jnp.where(mask, 1.0, 0.0).astype(BF)


def kernel(
    fine, down_w, conv_w, cot, fine_out, conv_out, down_out,
    x_mat, x_t, q, hs, ht, gp, gs, sums, part, part_in, r1, y1, r2, z1, r3, out,
    halo_s, halo_r, step_s, step_r, out_sem,
):
    gx, z = lax.axis_index("gx"), lax.axis_index("gy")
    px, py, c = gx // 8, (gx // 2) % 4, gx % 2

    def at(dx, dz):
        return ((gx + dx + 32) % 32, (z + dz + 8) % 8)

    def on_x(k):
        return ((((px + k) % 4) * 4 + py) * 2 + c, z)

    def on_y(k):
        return ((px * 4 + (py + k) % 4) * 2 + c, z)

    def on_z(k):
        return (gx, (z + k) % 8)

    partner = (gx + 1 - 2 * c, z)
    far = 4 * c - 2

    greeted = [at(dx, dz) for dx in (-1, 0, 1) for dz in (-1, 0, 1) if (dx, dz) != (0, 0)]
    greeted += [at(far * w, dz) for w in (1, -1) for dz in (-1, 0, 1)]
    greeted += [on_x(k) for k in (1, 2, 3)] + [on_y(k) for k in (1, 2, 3)]
    greeted += [on_z(k) for k in range(2, 7)]
    barrier = pltpu.get_barrier_semaphore()
    for device in greeted:
        pl.semaphore_signal(barrier, inc=1, device_id=device, device_id_type=MESH)

    started = []

    def send(src, dst, s_sem, r_sem, device):
        copy = pltpu.make_async_remote_copy(
            src_ref=src, dst_ref=dst, send_sem=s_sem, recv_sem=r_sem, device_id=device, device_id_type=MESH
        )
        copy.start()
        started.append(copy)
        return copy

    row, col = iotas(256)

    def target(r):
        group, j, k = r // 64, (r // 32) % 2, r % 32
        return (j * 2 + group // 2) * 64 + 2 * k + group % 2

    sort = ones_where(col == target(row))
    for a in range(2):
        for block in range(4):
            rows = fine[a, 4 * block : 4 * block + 4].reshape(256, 128)
            sorted_rows = dot(sort, rows).astype(BF)
            for group in range(4):
                lane = (4 * a + group) * 128
                x_mat[64 * block : 64 * block + 64, lane : lane + 128] = sorted_rows[64 * group : 64 * group + 64]
    hidden = dot(x_mat[...], down_w[...].reshape(1024, 256)).astype(BF)
    mine = 1 + c
    for half in range(2):
        q[mine, half, 32:288, :] = hidden[:, 128 * half : 128 * half + 128]

    pl.semaphore_wait(barrier, len(greeted))

    whole, low, high = pl.ds(32, 256), pl.ds(256, 32), pl.ds(32, 32)
    first, last = pl.ds(0, 32), pl.ds(288, 32)
    hidden_copies = []
    n = 0
    for dx, plane in ((1, 1 - c), (-1, 3 - c), (0, mine)):
        for dz, src, dst in ((0, whole, whole), (1, low, first), (-1, high, last)):
            if (dx, dz) != (0, 0):
                hidden_copies.append(
                    send(q.at[mine, :, src], q.at[plane, :, dst], halo_s.at[n], halo_r.at[n], at(dx, dz))
                )
                n += 1
    far_copies = []
    for dz, src, dst in ((0, whole, whole), (1, low, first), (-1, high, last)):
        far_copies.append(
            send(q.at[mine, c, src], q.at[3 - 3 * c, c, dst], halo_s.at[n], halo_r.at[n], at(far, dz))
        )
        n += 1

    r128, c128 = iotas(128)
    eye = ones_where(r128 == c128)
    for t in range(8):
        x_t[t] = dot_t(eye, x_mat[:, 128 * t : 128 * t + 128]).astype(BF)

    before = ones_where((col == row - 1) & (row % 32 != 0))
    after = ones_where((col == row + 1) & (row % 32 != 31))

    for copy in hidden_copies:
        copy.wait_recv()
    top, bottom, left, right = z > 0, z < 7, gx > 0, gx < 31
    for a, valid in ((0, left), (1, None), (2, right)):
        if valid is not None:
            q[c + a, :, 32:288] = jnp.where(valid, q[c + a, :, 32:288], jnp.zeros((2, 256, 128), BF))
        for rows, ok in ((slice(0, 32), top), (slice(288, 320), bottom)):
            both = ok if valid is None else jnp.logical_and(ok, valid)
            q[c + a, :, rows] = jnp.where(both, q[c + a, :, rows], jnp.zeros((2, 32, 128), BF))
    acc = None
    for a in range(3):
        plane = jnp.concatenate([q[c + a, 0], q[c + a, 1]], axis=1)
        for i, shift in ((0, before), (1, after)):
            hs[i, a, 0:256] = dot(shift, plane[0:256]).astype(BF)
            hs[i, a, 256:320] = dot(shift[0:64, 0:64], plane[256:320]).astype(BF)
        pieces = []
        for b in range(3):
            rows = slice(32 * b, 32 * b + 256)
            pieces += [hs[0, a, rows], plane[rows], hs[1, a, rows]]
        term = dot(jnp.concatenate(pieces, axis=1), conv_w[9 * a : 9 * a + 9].reshape(2304, 256))
        acc = term if acc is None else acc + term
    sig = jax.nn.sigmoid(acc)
    cotangent = cot[...].reshape(256, 256).astype(F32)
    gp[1, 32:288] = (cotangent * (sig * (1.0 + acc * (1.0 - sig)))).astype(BF)

    grad_copies = []
    for dx, plane in ((1, 0), (-1, 2), (0, 1)):
        for dz, src, dst in ((0, whole, whole), (1, low, first), (-1, high, last)):
            if (dx, dz) != (0, 0):
                grad_copies.append(
                    send(gp.at[1, src], gp.at[plane, dst], halo_s.at[n], halo_r.at[n], at(dx, dz))
                )
                n += 1

    for copy in far_copies:
        copy.wait_recv()
    far_plane = 3 - 3 * c
    far_ok = jnp.logical_and(gx + 2 - 4 * c >= 0, gx + 2 - 4 * c < 32)
    q[far_plane, c, 32:288] = jnp.where(far_ok, q[far_plane, c, 32:288], jnp.zeros((256, 128), BF))
    for rows, ok in ((slice(0, 32), top), (slice(288, 320), bottom)):
        both = jnp.logical_and(far_ok, ok)
        q[far_plane, c, rows] = jnp.where(both, q[far_plane, c, rows], jnp.zeros((32, 128), BF))
    for plane in range(4):
        for b in range(3):
            ht[b, plane] = dot_t(eye, q[plane, c, 32 * b : 32 * b + 256]).astype(BF)

    grad_copies[0].wait_recv()
    grad_copies[3].wait_recv()
    for a, valid in ((0, left), (2, right)):
        gp[a, 32:288] = jnp.where(valid, gp[a, 32:288], jnp.zeros((256, 256), BF))
    for a in range(3):
        for i, shift in ((0, after), (1, before)):
            gs[i, a, 32:288] = dot(shift, gp[a, 32:288]).astype(BF)

    class Stream:
        def __init__(self, index):
            self.i = index
            self.t0, self.n, self.x_first = STREAMS[index]
            self.f, self.s = (px, py) if self.x_first else (py, px)
            self.first, self.second = (on_x, on_y) if self.x_first else (on_y, on_x)

        def sems(self, slot):
            return step_s.at[self.i, slot], step_r.at[self.i, slot]

        def rows(self, f):
            return pl.ds(pl.multiple_of(32 * f, 32), 32)

        def tile(self, s):
            return pl.ds(pl.multiple_of(16 * (s % 2), 16), 16), pl.ds(pl.multiple_of(128 * (s // 2), 128), 128)

        def out_rows(self, f):
            return pl.ds(pl.multiple_of(c * 128 + 32 * f, 32), 32)

        def out_tile(self):
            lanes = pl.ds(pl.multiple_of(128 * (self.s // 2), 128), 128)
            return pl.ds(pl.multiple_of(c * 128 + 32 * self.f + 16 * (self.s % 2), 16), 16), lanes

        def start_first(self):
            self.c1 = []
            for k in (1, 2, 3):
                src = sums.at[self.t0 : self.t0 + self.n, self.rows((self.f + k) % 4)]
                dst = r1.at[self.i, k - 1, 0 : self.n]
                self.c1.append(send(src, dst, *self.sems(k - 1), self.first(k)))

        def start_second(self):
            total = sums[self.t0 : self.t0 + self.n, self.rows(self.f)].astype(F32)
            for k in (1, 2, 3):
                self.c1[k - 1].wait_recv()
                total = total + r1[self.i, k - 1, 0 : self.n].astype(F32)
            y1[self.i, 0 : self.n] = total.astype(BF)
            self.c2 = []
            for k in (1, 2, 3):
                rows, lanes = self.tile((self.s + k) % 4)
                src, dst = y1.at[self.i, 0 : self.n, rows, lanes], r2.at[self.i, k - 1, 0 : self.n]
                self.c2.append(send(src, dst, *self.sems(2 + k), self.second(k)))

        def start_third(self):
            rows, lanes = self.tile(self.s)
            total = y1[self.i, 0 : self.n, rows, lanes].astype(F32)
            for k in (1, 2, 3):
                self.c2[k - 1].wait_recv()
                total = total + r2[self.i, k - 1, 0 : self.n].astype(F32)
            z1[self.i, 0 : self.n] = total.astype(BF)
            if self.n < 8:
                z1[self.i, self.n : 8] = jnp.zeros((8 - self.n, 16, 128), BF)
            self.c3 = []
            for k in range(1, 8):
                self.c3.append(send(z1.at[self.i, (z + k) % 8], r3.at[self.i, k - 1], *self.sems(5 + k), on_z(k)))

        def gather_third(self):
            total = z1[self.i, z].astype(F32)
            for k in range(1, 8):
                self.c3[k - 1].wait_recv()
                total = total + r3[self.i, k - 1].astype(F32)
            rows, lanes = self.out_tile()
            out[self.i, z, rows, lanes] = total.astype(BF)
            self.c4 = []
            here = out.at[self.i, z, rows, lanes]
            for k in range(1, 8):
                self.c4.append(send(here, here, *self.sems(12 + k), on_z(k)))

        def gather_second(self):
            for copy in self.c4:
                copy.wait_recv()
            rows, lanes = self.out_tile()
            here = out.at[self.i, 0 : self.n, rows, lanes]
            self.c5 = [send(here, here, *self.sems(19 + k), self.second(k)) for k in (1, 2, 3)]

        def gather_first(self):
            for copy in self.c5:
                copy.wait_recv()
            here = out.at[self.i, 0 : self.n, self.out_rows(self.f)]
            self.c6 = [send(here, here, *self.sems(22 + k), self.first(k)) for k in (1, 2, 3)]
            self.c7 = [send(here, here, *self.sems(26), partner)]

        def gather_core(self):
            for k in (1, 2, 3):
                self.c6[k - 1].wait_recv()
                here = out.at[self.i, 0 : self.n, self.out_rows((self.f + 4 - k) % 4)]
                self.c7.append(send(here, here, *self.sems(26 + k), partner))

        def finish(self):
            for copy in self.c7:
                copy.wait_recv()
            if self.i < CONV_STREAMS:
                dst = conv_out.at[self.t0 : self.t0 + self.n]
                src = out.at[self.i, 0 : self.n]
                self.o = pltpu.make_async_copy(src, dst, out_sem.at[self.i])
                self.o.start()

    streams = [Stream(i) for i in range(len(STREAMS))]

    def grad_rows(s, p):
        a = p + 1 - c
        return gp[a, 32:288] if s == 1 else gs[s // 2, a, 32:288]

    both_planes = [jnp.concatenate([grad_rows(s, 0), grad_rows(s, 1)], axis=0) for s in range(3)]
    for stream in streams[:CONV_STREAMS]:
        for t in range(stream.t0, stream.t0 + stream.n):
            a, b, s = t // 9, (t // 3) % 3, t % 3
            lhs = jnp.concatenate([ht[b, a], ht[b, a + 1]], axis=1)
            sums[t] = dot(lhs, both_planes[s]).astype(BF)
        stream.start_first()

    for i, copy in enumerate(grad_copies):
        if i not in (0, 3):
            copy.wait_recv()
    for a, valid in ((0, left), (1, None), (2, right)):
        for rows, ok in ((slice(0, 32), top), (slice(288, 320), bottom)):
            both = ok if valid is None else jnp.logical_and(ok, valid)
            gp[a, rows] = jnp.where(both, gp[a, rows], jnp.zeros((32, 256), BF))
            for i, shift in ((0, after), (1, before)):
                gs[i, a, rows] = dot(shift[0:32, 0:32], gp[a, rows]).astype(BF)
    back = cotangent
    for a in range(3):
        for b in range(3):
            rows = slice(32 * (2 - b), 32 * (2 - b) + 256)
            for s in range(3):
                piece = gp[2 - a, rows] if s == 1 else gs[s // 2, 2 - a, rows]
                back = back + dot_t(piece, conv_w[9 * a + 3 * b + s])
    hidden_grad = back.astype(BF)
    for t in range(4):
        part[t] = dot(x_t[4 * (1 - c) + t], hidden_grad).astype(BF)
    down_copy = send(part, part_in, halo_s.at[n], halo_r.at[n], partner)
    n += 1

    for stream in streams[:CONV_STREAMS]:
        stream.start_second()

    unsort = ones_where(row == target(col))
    for a in range(2):
        flat = [dot_t(hidden_grad, down_w[4 * a + g]).astype(BF) for g in range(4)]
        for block in range(4):
            rows = jnp.concatenate([f[64 * block : 64 * block + 64] for f in flat], axis=0)
            fine_out[a, 4 * block : 4 * block + 4] = dot(unsort, rows).astype(BF).reshape(4, 64, 128)

    for stream in streams[:CONV_STREAMS]:
        stream.start_third()

    own = [dot(x_t[4 * c + t], hidden_grad) for t in range(4)]
    down_copy.wait_recv()
    for t in range(4):
        sums[27 + t] = (own[t] + part_in[t].astype(F32)).astype(BF)
    streams[4].start_first()

    for stream in streams[:CONV_STREAMS]:
        stream.gather_third()
    streams[4].start_second()
    for stream in streams[:CONV_STREAMS]:
        stream.gather_second()
    streams[4].start_third()
    for stream in streams[:CONV_STREAMS]:
        stream.gather_first()
    streams[4].gather_third()
    streams[4].gather_second()
    for stream in streams[:CONV_STREAMS]:
        stream.gather_core()
    streams[4].gather_first()
    for stream in streams[:CONV_STREAMS]:
        stream.finish()
    streams[4].gather_core()
    streams[4].finish()
    for core in range(2):
        down_out[4 * core : 4 * core + 4] = out[4, 0:4, 128 * core : 128 * core + 128]
    for copy in started:
        copy.wait_send()
    for stream in streams[:CONV_STREAMS]:
        stream.o.wait()


def on_device(fine_field, down_weight, conv_weight, coarse_cotangent):
    vmem = pl.BlockSpec(memory_space=pltpu.VMEM)
    count = len(STREAMS)
    return pl.pallas_call(
        kernel,
        out_shape=(
            jax.ShapeDtypeStruct(fine_field.shape, BF),
            jax.ShapeDtypeStruct(conv_weight.shape, BF),
            jax.ShapeDtypeStruct(down_weight.shape, BF),
        ),
        in_specs=[vmem] * 4,
        out_specs=(vmem, pl.BlockSpec(memory_space=pl.ANY), vmem),
        scratch_shapes=[
            pltpu.VMEM((256, 1024), BF),
            pltpu.VMEM((8, 128, 256), BF),
            pltpu.VMEM((4, 2, 320, 128), BF),
            pltpu.VMEM((2, 3, 320, 256), BF),
            pltpu.VMEM((3, 4, 128, 256), BF),
            pltpu.VMEM((3, 320, 256), BF),
            pltpu.VMEM((2, 3, 320, 256), BF),
            pltpu.VMEM((31, 128, 256), BF),
            pltpu.VMEM((4, 128, 256), BF),
            pltpu.VMEM((4, 128, 256), BF),
            pltpu.VMEM((count, 3, 8, 32, 256), BF),
            pltpu.VMEM((count, 8, 32, 256), BF),
            pltpu.VMEM((count, 3, 8, 16, 128), BF),
            pltpu.VMEM((count, 8, 16, 128), BF),
            pltpu.VMEM((count, 7, 16, 128), BF),
            pltpu.VMEM((count, 8, 256, 256), BF),
            pltpu.SemaphoreType.DMA((20,)),
            pltpu.SemaphoreType.DMA((20,)),
            pltpu.SemaphoreType.DMA((count, 30)),
            pltpu.SemaphoreType.DMA((count, 30)),
            pltpu.SemaphoreType.DMA((count,)),
        ],
        compiler_params=pltpu.CompilerParams(
            collective_id=0, has_side_effects=True, vmem_limit_bytes=48 * 1024 * 1024
        ),
        name="section_backward",
    )(fine_field, down_weight, conv_weight, coarse_cotangent)


def solution(mesh):
    in_specs = (P("gx", "gy", None, None), P(), P(), P("gx", "gy", None, None))
    out_specs = (P("gx", "gy", None, None), P(), P())
    return jax.shard_map(
        on_device, mesh=mesh, in_specs=in_specs, out_specs=out_specs, check_vma=False
    )
```

time: 233 us -> 81.3 us (0.35)
  blocking collectives: 150 us -> 0 us
  Pallas kernels: 0 us -> 74.1 us
  local copies, waits for them, and re-layouts: 40.9 us -> 6.36 us
  starting transfers between devices: 23.9 us -> 0 us
  matrix products: 9.26 us -> 0 us
  waiting for transfers between devices: 5.65 us -> 0 us
    psum x1 -> x0, blocking collectives: 150 us -> none  [on_device(): conv_total, down_total = lax.psum((conv_flat, down_vector), ('gx', 'gy'))]
    pallas_call x0 -> x1, Pallas kernels: none -> 74.1 us  [on_device(): pl.pallas_call(kernel, out_shape=(jax.ShapeDtypeStruct(fine_field.shape,...]
    ppermute x8 -> x0, starting transfers between devices: 23.9 us -> none  [the longest x4 14.1 us: padded_2(): before = lax.ppermute(last, axis, up)]
    unnamed x55 -> x9, local copies, waits for them, and re-layouts: 25 us -> 6.36 us
    reshape x5 -> x0, local copies, waits for them, and re-layouts: 9.56 us -> none  [the longest x1 6.4 us: on_device(): conv_weight_grad = conv_rounded.reshape(27, width, width)]
    dot_general x6 -> x0, matrix products: 9.26 us -> none  [the longest x1 6.09 us: on_device(): lax.dot_general(patches, pre_grad, (((0,), (0,)), ((), ())), preferred_el...]
    ppermute x8 -> x0, waiting for transfers between devices: 5.65 us -> none  [the longest x4 3.87 us: padded_2(): after = lax.ppermute(first, axis, down)]
    another operation x4 -> x0, local copies, waits for them, and re-layouts: 4.69 us -> none  [gather_taps(): stacked = jnp.stack(pieces, axis=3)]
  transfers between devices with their start and end apart: 8 -> 0, of which waited for: 3 -> 0; matrix products, arithmetic and copies ran while one was open for 9% -> 0% of each run, Pallas kernels for 0% -> 0%
where the time goes in v1:
time: 81.3 us; the launch traced here: 81.1 us
  Pallas kernels  74.1 us (91%)
  local copies, waits for them, and re-layouts  6.36 us (8%)
    pallas_call x1, Pallas kernels, on_device(): pl.pallas_call(kernel, out_shape=(jax.ShapeDtypeStruct(fine_field.shape,...  74.1 us
    unnamed x9, local copies, waits for them, and re-layouts  6.36 us

profile of v1, /device:TPU:1, one launch (start us, length us, event | category | flops | bytes accessed | tf_op | source)
XLA Modules:
  0.0 81.1 jit_solution(15479741595412428256)
XLA Ops:
  0.6 0.0 copy-start
  0.6 1.0 %copy-done = bf16[2,16,64,128]{3,2,1,0:T(8,128)(2,1)S(1)} copy-done((bf16[2,16,64,128]{3,2,1,0:T(8,128)(2,1)S(1)}, bf16[2,16,64,128]{3,2,1,0:T(8,128)(2,1)}, u32[]{:S(2)}) %copy-start) | copy-done | bytes 524312
  1.7 0.0 copy-start.1
  1.7 1.0 %copy-done.1 = bf16[8,128,256]{2,1,0:T(8,128)(2,1)S(1)} copy-done((bf16[8,128,256]{2,1,0:T(8,128)(2,1)S(1)}, bf16[8,128,256]{2,1,0:T(8,128)(2,1)}, u32[]{:S(2)}) %copy-start.1) | copy-done | bytes 524312
  2.7 0.0 copy-start.2
  2.7 0.9 %copy-done.2 = bf16[1,8,32,256]{3,2,1,0:T(8,128)(2,1)S(1)} copy-done((bf16[1,8,32,256]{3,2,1,0:T(8,128)(2,1)S(1)}, bf16[1,8,32,256]{3,2,1,0:T(8,128)(2,1)}, u32[]{:S(2)}) %copy-start.2) | copy-done | bytes 131096
  3.6 74.1 %section_backward.1 = (bf16[2,16,64,128]{3,2,1,0:T(8,128)(2,1)S(1)}, bf16[27,256,256]{2,1,0:T(8,128)(2,1)S(1)}, bf16[8,128,256]{2,1,0:T(8,128)(2,1)S(1)}) custom-call(bf16[2,16,64,128]{3,2,1,0:T(8,128)(2,1)S(1)} %copy-done, bf16[8,128,256]{2,1,0:T(8,128)(2,1)S(1)} %copy-done.1, bf16[27,256,256]{2,1,0:T(8,128)(2,1)} %conv_w.1, ...), custom_call_target="tpu_custom_call" | custom-call | tf_op jit(solution)/shard_map/section_backward/pallas_call | solution.py:353
  77.7 0.8 copy.10
  78.5 1.8 %copy.11 = bf16[27,256,256]{2,1,0:T(8,128)(2,1)} copy(bf16[27,256,256]{2,1,0:T(8,128)(2,1)S(1)} %get-tuple-element.7) | data formatting | bytes 7077888
  80.3 0.8 copy.12
Async XLA Ops:
  0.6 1.0 %copy-start = (bf16[2,16,64,128]{3,2,1,0:T(8,128)(2,1)S(1)}, bf16[2,16,64,128]{3,2,1,0:T(8,128)(2,1)}, u32[]{:S(2)}) copy-start(bf16[2,16,64,128]{3,2,1,0:T(8,128)(2,1)} %fine.1) | copy-start | bytes 1572868
  1.7 1.0 %copy-start.1 = (bf16[8,128,256]{2,1,0:T(8,128)(2,1)S(1)}, bf16[8,128,256]{2,1,0:T(8,128)(2,1)}, u32[]{:S(2)}) copy-start(bf16[8,128,256]{2,1,0:T(8,128)(2,1)} %down_w.1) | copy-start | bytes 1572868
  2.7 0.9 %copy-start.2 = (bf16[1,8,32,256]{3,2,1,0:T(8,128)(2,1)S(1)}, bf16[1,8,32,256]{3,2,1,0:T(8,128)(2,1)}, u32[]{:S(2)}) copy-start(bf16[1,8,32,256]{3,2,1,0:T(8,128)(2,1)} %cot.1) | copy-start | bytes 393220

commit v2 on v1

--- a/solution.py
+++ b/solution.py
@@ -30,9 +30,9 @@
 
 
 def kernel(
-    fine, down_w, conv_w, cot, fine_out, conv_out, down_out,
-    x_mat, x_t, q, hs, ht, gp, gs, sums, part, part_in, r1, y1, r2, z1, r3, out,
-    halo_s, halo_r, step_s, step_r, out_sem,
+    fine_in, down_in, conv_in, cot_in, fine_out, conv_out, down_out,
+    fine, down_w, conv_w, cot, x_mat, x_t, q, hs, ht, gp, gs, sums, part, part_in, r1, y1, r2, z1, r3, out,
+    halo_s, halo_r, step_s, step_r, out_sem, in_sem,
 ):
     gx, z = lax.axis_index("gx"), lax.axis_index("gy")
     px, py, c = gx // 8, (gx // 2) % 4, gx % 2
@@ -50,10 +50,15 @@
         return (gx, (z + k) % 8)
 
     partner = (gx + 1 - 2 * c, z)
-    far = 4 * c - 2
+    other = 2 * c - 1
+
+    loads = []
+    for i, (src, dst) in enumerate(((fine_in, fine), (down_in, down_w), (cot_in, cot), (conv_in, conv_w))):
+        load = pltpu.make_async_copy(src, dst, in_sem.at[i])
+        load.start()
+        loads.append(load)
 
     greeted = [at(dx, dz) for dx in (-1, 0, 1) for dz in (-1, 0, 1) if (dx, dz) != (0, 0)]
-    greeted += [at(far * w, dz) for w in (1, -1) for dz in (-1, 0, 1)]
     greeted += [on_x(k) for k in (1, 2, 3)] + [on_y(k) for k in (1, 2, 3)]
     greeted += [on_z(k) for k in range(2, 7)]
     barrier = pltpu.get_barrier_semaphore()
@@ -73,10 +78,16 @@
     row, col = iotas(256)
 
     def target(r):
-        group, j, k = r // 64, (r // 32) % 2, r % 32
-        return (j * 2 + group // 2) * 64 + 2 * k + group % 2
+        group, j, k = r >> 6, (r >> 5) & 1, r & 31
+        return (j * 2 + (group >> 1)) * 64 + 2 * k + (group & 1)
 
     sort = ones_where(col == target(row))
+    before = ones_where((col == row - 1) & ((row & 31) != 0))
+    after = ones_where((col == row + 1) & ((row & 31) != 31))
+    r128, c128 = iotas(128)
+    eye = ones_where(r128 == c128)
+    loads[0].wait()
+    loads[1].wait()
     for a in range(2):
         for block in range(4):
             rows = fine[a, 4 * block : 4 * block + 4].reshape(256, 128)
@@ -93,39 +104,41 @@
 
     whole, low, high = pl.ds(32, 256), pl.ds(256, 32), pl.ds(32, 32)
     first, last = pl.ds(0, 32), pl.ds(288, 32)
-    hidden_copies = []
+    sides = ((-other, 1 + c, 2 * c), (other, 3 * (1 - c), 2 - 2 * c), (0, 1 + c, 1))
+    shifts = ((0, whole, whole), (1, low, first), (-1, high, last))
     n = 0
-    for dx, plane in ((1, 1 - c), (-1, 3 - c), (0, mine)):
-        for dz, src, dst in ((0, whole, whole), (1, low, first), (-1, high, last)):
-            if (dx, dz) != (0, 0):
-                hidden_copies.append(
-                    send(q.at[mine, :, src], q.at[plane, :, dst], halo_s.at[n], halo_r.at[n], at(dx, dz))
-                )
-                n += 1
-    far_copies = []
-    for dz, src, dst in ((0, whole, whole), (1, low, first), (-1, high, last)):
-        far_copies.append(
-            send(q.at[mine, c, src], q.at[3 - 3 * c, c, dst], halo_s.at[n], halo_r.at[n], at(far, dz))
-        )
-        n += 1
-
-    r128, c128 = iotas(128)
-    eye = ones_where(r128 == c128)
+
+    def halo(source_of, target_of):
+        nonlocal n
+        copies = []
+        for dz, src, dst in shifts:
+            for side in range(3):
+                if (dz, side) != (0, 2):
+                    dx = sides[side][0]
+                    sent = send(source_of(src), target_of(side, dst), halo_s.at[n], halo_r.at[n], at(dx, dz))
+                    copies.append(sent)
+                    n += 1
+        return copies
+
+    hidden_copies = halo(lambda rows: q.at[mine, :, rows], lambda side, rows: q.at[sides[side][1], :, rows])
     for t in range(8):
         x_t[t] = dot_t(eye, x_mat[:, 128 * t : 128 * t + 128]).astype(BF)
 
-    before = ones_where((col == row - 1) & (row % 32 != 0))
-    after = ones_where((col == row + 1) & (row % 32 != 31))
-
     for copy in hidden_copies:
         copy.wait_recv()
-    top, bottom, left, right = z > 0, z < 7, gx > 0, gx < 31
-    for a, valid in ((0, left), (1, None), (2, right)):
-        if valid is not None:
-            q[c + a, :, 32:288] = jnp.where(valid, q[c + a, :, 32:288], jnp.zeros((2, 256, 128), BF))
-        for rows, ok in ((slice(0, 32), top), (slice(288, 320), bottom)):
+    top, bottom = z > 0, z < 7
+    other_ok = jnp.logical_and(gx + other >= 0, gx + other < 32)
+    far_plane = 3 * c
+    q[far_plane, :, 32:288] = jnp.where(other_ok, q[far_plane, :, 32:288], jnp.zeros((2, 256, 128), BF))
+    edges = ((slice(0, 32), top), (slice(288, 320), bottom))
+    for plane, valid in ((1, None), (2, None), (far_plane, other_ok)):
+        for rows, ok in edges:
             both = ok if valid is None else jnp.logical_and(ok, valid)
-            q[c + a, :, rows] = jnp.where(both, q[c + a, :, rows], jnp.zeros((2, 32, 128), BF))
+            q[plane, :, rows] = jnp.where(both, q[plane, :, rows], jnp.zeros((2, 32, 128), BF))
+    beyond = q.at[far_plane, 1 - c]
+    far_copy = send(beyond, beyond, halo_s.at[n], halo_r.at[n], partner)
+    n += 1
+    loads[3].wait()
     acc = None
     for a in range(3):
         plane = jnp.concatenate([q[c + a, 0], q[c + a, 1]], axis=1)
@@ -139,37 +152,22 @@
         term = dot(jnp.concatenate(pieces, axis=1), conv_w[9 * a : 9 * a + 9].reshape(2304, 256))
         acc = term if acc is None else acc + term
     sig = jax.nn.sigmoid(acc)
+    loads[2].wait()
     cotangent = cot[...].reshape(256, 256).astype(F32)
     gp[1, 32:288] = (cotangent * (sig * (1.0 + acc * (1.0 - sig)))).astype(BF)
 
-    grad_copies = []
-    for dx, plane in ((1, 0), (-1, 2), (0, 1)):
-        for dz, src, dst in ((0, whole, whole), (1, low, first), (-1, high, last)):
-            if (dx, dz) != (0, 0):
-                grad_copies.append(
-                    send(gp.at[1, src], gp.at[plane, dst], halo_s.at[n], halo_r.at[n], at(dx, dz))
-                )
-                n += 1
-
-    for copy in far_copies:
-        copy.wait_recv()
-    far_plane = 3 - 3 * c
-    far_ok = jnp.logical_and(gx + 2 - 4 * c >= 0, gx + 2 - 4 * c < 32)
-    q[far_plane, c, 32:288] = jnp.where(far_ok, q[far_plane, c, 32:288], jnp.zeros((256, 128), BF))
-    for rows, ok in ((slice(0, 32), top), (slice(288, 320), bottom)):
-        both = jnp.logical_and(far_ok, ok)
-        q[far_plane, c, rows] = jnp.where(both, q[far_plane, c, rows], jnp.zeros((32, 128), BF))
+    grad_copies = halo(lambda rows: gp.at[1, rows], lambda side, rows: gp.at[sides[side][2], rows])
+    far_copy.wait_recv()
     for plane in range(4):
         for b in range(3):
             ht[b, plane] = dot_t(eye, q[plane, c, 32 * b : 32 * b + 256]).astype(BF)
+    for i, shift in ((0, after), (1, before)):
+        gs[i, 1, 32:288] = dot(shift, gp[1, 32:288]).astype(BF)
 
     grad_copies[0].wait_recv()
-    grad_copies[3].wait_recv()
-    for a, valid in ((0, left), (2, right)):
-        gp[a, 32:288] = jnp.where(valid, gp[a, 32:288], jnp.zeros((256, 256), BF))
-    for a in range(3):
-        for i, shift in ((0, after), (1, before)):
-            gs[i, a, 32:288] = dot(shift, gp[a, 32:288]).astype(BF)
+    near = 2 - 2 * c
+    for i, shift in ((0, after), (1, before)):
+        gs[i, near, 32:288] = dot(shift, gp[near, 32:288]).astype(BF)
 
     class Stream:
         def __init__(self, index):
@@ -281,15 +279,18 @@
             sums[t] = dot(lhs, both_planes[s]).astype(BF)
         stream.start_first()
 
-    for i, copy in enumerate(grad_copies):
-        if i not in (0, 3):
-            copy.wait_recv()
-    for a, valid in ((0, left), (1, None), (2, right)):
-        for rows, ok in ((slice(0, 32), top), (slice(288, 320), bottom)):
+    for copy in grad_copies[1:]:
+        copy.wait_recv()
+    away = 2 * c
+    gp[away, 32:288] = jnp.where(other_ok, gp[away, 32:288], jnp.zeros((256, 256), BF))
+    for i, shift in ((0, after), (1, before)):
+        gs[i, away, 32:288] = dot(shift, gp[away, 32:288]).astype(BF)
+    for plane, valid in ((1, None), (near, None), (away, other_ok)):
+        for rows, ok in edges:
             both = ok if valid is None else jnp.logical_and(ok, valid)
-            gp[a, rows] = jnp.where(both, gp[a, rows], jnp.zeros((32, 256), BF))
+            gp[plane, rows] = jnp.where(both, gp[plane, rows], jnp.zeros((32, 256), BF))
             for i, shift in ((0, after), (1, before)):
-                gs[i, a, rows] = dot(shift[0:32, 0:32], gp[a, rows]).astype(BF)
+                gs[i, plane, rows] = dot(shift[0:32, 0:32], gp[plane, rows]).astype(BF)
     back = cotangent
     for a in range(3):
         for b in range(3):
@@ -347,19 +348,35 @@
         stream.o.wait()
 
 
+def deliver(fine, conv, down, fine_out, conv_out, down_out, sems):
+    copies = []
+    for i, (src, dst) in enumerate(((conv, conv_out), (fine, fine_out), (down, down_out))):
+        copy = pltpu.make_async_copy(src, dst, sems.at[i])
+        copy.start()
+        copies.append(copy)
+    for copy in copies:
+        copy.wait()
+
+
 def on_device(fine_field, down_weight, conv_weight, coarse_cotangent):
     vmem = pl.BlockSpec(memory_space=pltpu.VMEM)
     count = len(STREAMS)
-    return pl.pallas_call(
+    operands = (fine_field, down_weight, conv_weight, coarse_cotangent)
+    operands = [pltpu.with_memory_space_constraint(x, pltpu.HBM) for x in operands]
+    results = pl.pallas_call(
         kernel,
         out_shape=(
             jax.ShapeDtypeStruct(fine_field.shape, BF),
             jax.ShapeDtypeStruct(conv_weight.shape, BF),
             jax.ShapeDtypeStruct(down_weight.shape, BF),
         ),
-        in_specs=[vmem] * 4,
+        in_specs=[pl.BlockSpec(memory_space=pltpu.HBM)] * 4,
         out_specs=(vmem, pl.BlockSpec(memory_space=pl.ANY), vmem),
         scratch_shapes=[
+            pltpu.VMEM(fine_field.shape, BF),
+            pltpu.VMEM(down_weight.shape, BF),
+            pltpu.VMEM(conv_weight.shape, BF),
+            pltpu.VMEM(coarse_cotangent.shape, BF),
             pltpu.VMEM((256, 1024), BF),
             pltpu.VMEM((8, 128, 256), BF),
             pltpu.VMEM((4, 2, 320, 128), BF),
@@ -381,12 +398,23 @@
             pltpu.SemaphoreType.DMA((count, 30)),
             pltpu.SemaphoreType.DMA((count, 30)),
             pltpu.SemaphoreType.DMA((count,)),
+            pltpu.SemaphoreType.DMA((4,)),
         ],
         compiler_params=pltpu.CompilerParams(
-            collective_id=0, has_side_effects=True, vmem_limit_bytes=48 * 1024 * 1024
+            collective_id=0, has_side_effects=True, vmem_limit_bytes=36 * 1024 * 1024
         ),
         name="section_backward",
-    )(fine_field, down_weight, conv_weight, coarse_cotangent)
+    )(*operands)
+    hbm = pl.BlockSpec(memory_space=pltpu.HBM)
+    return pl.pallas_call(
+        deliver,
+        out_shape=tuple(jax.ShapeDtypeStruct(r.shape, r.dtype) for r in results),
+        in_specs=[vmem] * 3,
+        out_specs=(hbm, hbm, hbm),
+        scratch_shapes=[pltpu.SemaphoreType.DMA((3,))],
+        compiler_params=pltpu.CompilerParams(vmem_limit_bytes=1024 * 1024),
+        name="deliver",
+    )(*[pltpu.with_memory_space_constraint(r, pltpu.VMEM) for r in results])
 
 
 def solution(mesh):

time: 81.3 us -> 73.2 us (0.900)
  local copies, waits for them, and re-layouts: 6.36 us -> 0 us
  Pallas kernels: 74.1 us -> 72.5 us
    unnamed x9 -> x0, local copies, waits for them, and re-layouts: 6.36 us -> none
    pallas_call x1, Pallas kernels: 74.1 us -> 70.3 us  [on_device(): pl.pallas_call(kernel, out_shape=(jax.ShapeDtypeStruct(fine_field.shape,...]
    pallas_call x0 -> x1, Pallas kernels: none -> 2.16 us  [on_device(): pl.pallas_call(deliver, out_shape=tuple((jax.ShapeDtypeStruct(r.shape, r....]
where the time goes in v2:
time: 73.2 us; the launch traced here: 73.1 us
  Pallas kernels  72.5 us (99%)
    pallas_call x1, Pallas kernels, on_device(): pl.pallas_call(kernel, out_shape=(jax.ShapeDtypeStruct(fine_field.shape,...  70.3 us
    pallas_call x1, Pallas kernels, on_device(): pl.pallas_call(deliver, out_shape=tuple((jax.ShapeDtypeStruct(r.shape, r....  2.16 us

profile of v2, /device:TPU:1, one launch (start us, length us, event | category | flops | bytes accessed | tf_op | source)
XLA Modules:
  0.0 73.1 jit_solution(4699974300531555394)
XLA Ops:
  0.6 70.3 %section_backward.1 = (bf16[2,16,64,128]{3,2,1,0:T(8,128)(2,1)S(1)}, bf16[27,256,256]{2,1,0:T(8,128)(2,1)S(1)}, bf16[8,128,256]{2,1,0:T(8,128)(2,1)S(1)}) custom-call(bf16[2,16,64,128]{3,2,1,0:T(8,128)(2,1)} %fine_in.1, bf16[8,128,256]{2,1,0:T(8,128)(2,1)} %down_in.1, bf16[27,256,256]{2,1,0:T(8,128)(2,1)} %conv_in.1, bf16[1,8,32,256]{3,2,1,0:T(8,128)(2,1)} %cot_in.1), custom_call_target="tpu_custom_call" | custom-call | tf_op jit(solution)/shard_map/section_backward/pallas_call | solution.py:366
  71.0 2.2 %deliver.1 = (bf16[2,16,64,128]{3,2,1,0:T(8,128)(2,1)}, bf16[27,256,256]{2,1,0:T(8,128)(2,1)}, bf16[8,128,256]{2,1,0:T(8,128)(2,1)}) custom-call(bf16[2,16,64,128]{3,2,1,0:T(8,128)(2,1)S(1)} %get-tuple-element.6.fine, bf16[27,256,256]{2,1,0:T(8,128)(2,1)S(1)} %get-tuple-element.7.conv, bf16[8,128,256]{2,1,0:T(8,128)(2,1)S(1)} %get-tuple-element.8.down), custom_call_target="tpu_custom_call" | custom-call | tf_op jit(solution)/shard_map/deliver/pallas_call | solution.py:409

commit v3 on v2

v3 whole, which is shorter than its diff:
```python
import math

import jax
import jax.numpy as jnp
from jax import lax
from jax.experimental import pallas as pl
from jax.experimental.pallas import tpu as pltpu
from jax.sharding import PartitionSpec as P

MESH = pl.DeviceIdType.MESH
BF = jnp.bfloat16
F32 = jnp.float32

GROUPS = (((0, 4), (4, 4)), ((8, 4), (12, 4)), ((16, 4), (20, 4)), ((24, 3), (27, 4)))
CONV_TAPS = 27
SEMAPHORES = 54


def dot(a, b):
    return jnp.dot(a, b, preferred_element_type=F32)


def dot_t(a, b):
    return lax.dot_general(a, b, (((1,), (1,)), ((), ())), preferred_element_type=F32)


def iotas(n):
    return lax.broadcasted_iota(jnp.int32, (n, n), 0), lax.broadcasted_iota(jnp.int32, (n, n), 1)


def ones_where(mask):
    return jnp.where(mask, 1.0, 0.0).astype(BF)


def kernel(
    fine_in, down_in, conv_in, cot_in, fine_out, out,
    fine, down_w, conv_w, cot, x_mat, x_t, q, hs, ht, gp, gs, sums, part, part_in, r1, y1, r2, z1, r3, measure, sems,
):
    gx, z = lax.axis_index("gx"), lax.axis_index("gy")
    px, py, c = gx // 8, (gx // 2) % 4, gx % 2

    def at(dx, dz):
        return ((gx + dx + 32) % 32, (z + dz + 8) % 8)

    def on_x(k):
        return ((((px + k) % 4) * 4 + py) * 2 + c, z)

    def on_y(k):
        return ((px * 4 + (py + k) % 4) * 2 + c, z)

    def on_z(k):
        return (gx, (z + k) % 8)

    partner = (gx + 1 - 2 * c, z)
    other = 2 * c - 1

    names, amounts = {}, {}

    def sem(name):
        return sems.at[names.setdefault(name, len(names))]

    def count(name, ref):
        amounts[name] = amounts.get(name, 0) + math.prod(ref.shape) // 2048

    def wait(name):
        tiles = measure.at[0 : amounts.pop(name)]
        pltpu.make_async_copy(tiles, tiles, sem(name)).wait()

    def wait_all():
        for name in list(amounts):
            wait(name)

    def load(src, dst, name):
        count(name, src)
        pltpu.make_async_copy(src, dst, sem(name)).start()

    def send(src, dst, sent, received, device):
        count(sent, src)
        count(received, src)
        pltpu.make_async_remote_copy(
            src_ref=src, dst_ref=dst, send_sem=sem(sent), recv_sem=sem(received), device_id=device, device_id_type=MESH
        ).start()

    load(fine_in, fine, "fine")
    load(down_in, down_w, "fine")
    load(cot_in, cot, "cot")
    load(conv_in, conv_w, "conv")

    greeted = [at(dx, dz) for dx in (-1, 0, 1) for dz in (-1, 0, 1) if (dx, dz) != (0, 0)]
    greeted += [on_x(k) for k in (1, 2, 3)] + [on_y(k) for k in (1, 2, 3)]
    greeted += [on_z(k) for k in range(2, 7)]
    barrier = pltpu.get_barrier_semaphore()
    for device in greeted:
        pl.semaphore_signal(barrier, inc=1, device_id=device, device_id_type=MESH)

    row, col = iotas(256)

    def target(r):
        group, j, k = r >> 6, (r >> 5) & 1, r & 31
        return (j * 2 + (group >> 1)) * 64 + 2 * k + (group & 1)

    sort = ones_where(col == target(row))
    before = ones_where((col == row - 1) & ((row & 31) != 0))
    after = ones_where((col == row + 1) & ((row & 31) != 31))
    r128, c128 = iotas(128)
    eye = ones_where(r128 == c128)
    wait("fine")
    for a in range(2):
        for block in range(4):
            rows = fine[a, 4 * block : 4 * block + 4].reshape(256, 128)
            sorted_rows = dot(sort, rows).astype(BF)
            for group in range(4):
                lane = (4 * a + group) * 128
                x_mat[64 * block : 64 * block + 64, lane : lane + 128] = sorted_rows[64 * group : 64 * group + 64]
    hidden = dot(x_mat[...], down_w[...].reshape(1024, 256)).astype(BF)
    mine = 1 + c
    for half in range(2):
        q[mine, half, 32:288, :] = hidden[:, 128 * half : 128 * half + 128]

    pl.semaphore_wait(barrier, len(greeted))

    whole, low, high = pl.ds(32, 256), pl.ds(256, 32), pl.ds(32, 32)
    first, last = pl.ds(0, 32), pl.ds(288, 32)
    sides = ((-other, 1 + c, 2 * c), (other, 3 * (1 - c), 2 - 2 * c), (0, 1 + c, 1))
    shifts = ((0, whole, whole), (1, low, first), (-1, high, last))

    def halo(kind, source_of, target_of):
        for dz, src, dst in shifts[1:] + shifts[:1]:
            for side in (2, 0, 1):
                if (dz, side) != (0, 2):
                    name = (kind, side, dz == 0 and kind == "grad")
                    send(source_of(src), target_of(side, dst), "halo sent", name, at(sides[side][0], dz))

    halo("hidden", lambda rows: q.at[mine, :, rows], lambda side, rows: q.at[sides[side][1], :, rows])
    for t in range(8):
        x_t[t] = dot_t(eye, x_mat[:, 128 * t : 128 * t + 128]).astype(BF)

    top, bottom = z > 0, z < 7
    other_ok = jnp.logical_and(gx + other >= 0, gx + other < 32)
    far_plane = 3 * c
    edges = ((slice(0, 32), top), (slice(288, 320), bottom))

    def clear(ref, index, rows, ok):
        old = ref[index + (rows,)]
        ref[index + (rows,)] = jnp.where(ok, old, jnp.zeros(old.shape, BF))

    acc = None
    for role, plane, a, side in ((0, mine, 1, 2), (1, 2 - c, 2 - 2 * c, 0), (2, far_plane, 2 * c, 1)):
        wait(("hidden", side, False))
        for rows, ok in edges:
            clear(q, (plane, slice(None)), rows, ok if side != 1 else jnp.logical_and(ok, other_ok))
        if side == 1:
            clear(q, (plane, slice(None)), slice(32, 288), other_ok)
            beyond = q.at[far_plane, 1 - c]
            send(beyond, beyond, "halo sent", "far", partner)
        elif side == 2:
            wait("conv")
        rows_of = jnp.concatenate([q[plane, 0], q[plane, 1]], axis=1)
        for i, shift in ((0, before), (1, after)):
            hs[i, role, 0:256] = dot(shift, rows_of[0:256]).astype(BF)
            hs[i, role, 256:320] = dot(shift[0:64, 0:64], rows_of[256:320]).astype(BF)
        pieces = []
        for b in range(3):
            rows = slice(32 * b, 32 * b + 256)
            pieces += [hs[0, role, rows], rows_of[rows], hs[1, role, rows]]
        taps = conv_w[pl.ds(9 * a, 9)].reshape(2304, 256)
        term = dot(jnp.concatenate(pieces, axis=1), taps)
        acc = term if acc is None else acc + term
    sig = jax.nn.sigmoid(acc)
    wait("cot")
    cotangent = cot[...].reshape(256, 256).astype(F32)
    gp[1, 32:288] = (cotangent * (sig * (1.0 + acc * (1.0 - sig)))).astype(BF)

    halo("grad", lambda rows: gp.at[1, rows], lambda side, rows: gp.at[sides[side][2], rows])
    wait("far")
    for plane in range(4):
        for b in range(3):
            ht[b, plane] = dot_t(eye, q[plane, c, 32 * b : 32 * b + 256]).astype(BF)
    for i, shift in ((0, after), (1, before)):
        gs[i, 1, 32:288] = dot(shift, gp[1, 32:288]).astype(BF)

    wait(("grad", 0, True))
    near = 2 - 2 * c
    for i, shift in ((0, after), (1, before)):
        gs[i, near, 32:288] = dot(shift, gp[near, 32:288]).astype(BF)

    def row_block(f):
        return pl.ds(pl.multiple_of(32 * f, 32), 32)

    class Stream:
        def __init__(self, group, half):
            self.i, self.group = 2 * group + half, group
            self.t0, self.n = GROUPS[group][half]
            self.tile0 = self.t0 - 8 * group
            self.f, self.s = (px, py) if half == 0 else (py, px)
            self.first, self.second = (on_x, on_y) if half == 0 else (on_y, on_x)
            self.row = c * 128 + 32 * self.f + 16 * (self.s % 2)
            self.lane = 128 * (self.s // 2)

        def send(self, src, dst, name, device):
            send(src, dst, ("sent", self.group), (name, self.group), device)

        def tile(self, s):
            return pl.ds(pl.multiple_of(16 * (s % 2), 16), 16), pl.ds(pl.multiple_of(128 * (s // 2), 128), 128)

        def out_rows(self, f):
            rows = pl.ds(pl.multiple_of(c * 128 + 32 * f, 32), 32)
            return out.at[self.t0 : self.t0 + self.n, rows]

        def start_first(self):
            for k in (1, 3, 2):
                src = sums.at[self.t0 : self.t0 + self.n, row_block((self.f + k) % 4)]
                self.send(src, r1.at[self.i, k - 1, 0 : self.n], "first", self.first(k))

        def start_second(self):
            total = sums[self.t0 : self.t0 + self.n, row_block(self.f)].astype(F32)
            for k in range(3):
                total = total + r1[self.i, k, 0 : self.n].astype(F32)
            y1[self.i, 0 : self.n] = total.astype(BF)
            for k in (1, 3, 2):
                rows, lanes = self.tile((self.s + k) % 4)
                src = y1.at[self.i, 0 : self.n, rows, lanes]
                self.send(src, r2.at[self.i, k - 1, 0 : self.n], "second", self.second(k))

        def sum_second(self):
            rows, lanes = self.tile(self.s)
            total = y1[self.i, 0 : self.n, rows, lanes].astype(F32)
            for k in range(3):
                total = total + r2[self.i, k, 0 : self.n].astype(F32)
            z1[self.group, self.tile0 : self.tile0 + self.n] = total.astype(BF)

        def gather_second(self):
            rows = pl.ds(pl.multiple_of(self.row, 16), 16)
            lanes = pl.ds(pl.multiple_of(self.lane, 128), 128)
            here = out.at[self.t0 : self.t0 + self.n, rows, lanes]
            for k in (1, 3, 2):
                self.send(here, here, "gather second", self.second(k))

        def gather_first(self):
            here = self.out_rows(self.f)
            for k in (1, 3, 2):
                self.send(here, here, ("gather first", k), self.first(k))
            self.send(here, here, "core", partner)

        def gather_core(self, k):
            here = self.out_rows((self.f + 4 - k) % 4)
            self.send(here, here, "core", partner)

    class Group:
        def __init__(self, index):
            self.i = index
            self.streams = [Stream(index, half) for half in range(2)]

        def send(self, src, dst, name, device):
            send(src, dst, ("sent", self.i), (name, self.i), device)

        def start_first(self):
            for stream in self.streams:
                stream.start_first()

        def start_second(self):
            wait(("first", self.i))
            for stream in self.streams:
                stream.start_second()

        def start_third(self):
            wait(("second", self.i))
            for stream in self.streams:
                stream.sum_second()
            end = self.streams[1].tile0 + self.streams[1].n
            if end < 8:
                z1[self.i, end:8] = jnp.zeros((8 - end, 16, 128), BF)
            for k in (4, 3, 5, 2, 6, 1, 7):
                self.send(z1.at[self.i, (z + k) % 8], r3.at[self.i, k - 1], "third", on_z(k))

        def gather_third(self):
            wait(("third", self.i))
            total = z1[self.i, z].astype(F32)
            for k in range(7):
                total = total + r3[self.i, k].astype(F32)
            a, b = self.streams
            later = (z + 8 - b.tile0) // 8
            rows = pl.ds(pl.multiple_of(a.row + later * (b.row - a.row), 16), 16)
            lanes = pl.ds(pl.multiple_of(a.lane + later * (b.lane - a.lane), 128), 128)
            out[8 * self.i + z, rows, lanes] = total.astype(BF)
            here = out.at[8 * self.i + z, rows, lanes]
            for k in (4, 3, 5, 2, 6, 1, 7):
                self.send(here, here, "gather third", on_z(k))

        def gather_second(self):
            wait(("gather third", self.i))
            for stream in self.streams:
                stream.gather_second()

        def gather_first(self):
            wait(("gather second", self.i))
            for stream in self.streams:
                stream.gather_first()

        def gather_core(self):
            for k in (1, 3, 2):
                wait((("gather first", k), self.i))
                for stream in self.streams:
                    stream.gather_core(k)

        def finish(self):
            wait(("core", self.i))

    groups = [Group(i) for i in range(len(GROUPS))]

    def grad_rows(s, p):
        a = p + 1 - c
        return gp[a, 32:288] if s == 1 else gs[s // 2, a, 32:288]

    both_planes = [jnp.concatenate([grad_rows(s, 0), grad_rows(s, 1)], axis=0) for s in range(3)]
    for t in range(CONV_TAPS):
        a, b, s = t // 9, (t // 3) % 3, t % 3
        lhs = jnp.concatenate([ht[b, a], ht[b, a + 1]], axis=1)
        sums[t] = dot(lhs, both_planes[s]).astype(BF)
        if t % 8 == 7:
            groups[t // 8].start_first()

    for name in (("grad", 2, False), ("grad", 0, False), ("grad", 1, False), ("grad", 1, True)):
        wait(name)
    away = 2 * c
    clear(gp, (away,), slice(32, 288), other_ok)
    for i, shift in ((0, after), (1, before)):
        gs[i, away, 32:288] = dot(shift, gp[away, 32:288]).astype(BF)
    for plane, valid in ((1, None), (near, None), (away, other_ok)):
        for rows, ok in edges:
            clear(gp, (plane,), rows, ok if valid is None else jnp.logical_and(ok, valid))
            for i, shift in ((0, after), (1, before)):
                gs[i, plane, rows] = dot(shift[0:32, 0:32], gp[plane, rows]).astype(BF)
    back = cotangent
    for a in range(3):
        for b in range(3):
            rows = slice(32 * (2 - b), 32 * (2 - b) + 256)
            for s in range(3):
                piece = gp[2 - a, rows] if s == 1 else gs[s // 2, 2 - a, rows]
                back = back + dot_t(piece, conv_w[9 * a + 3 * b + s])
    hidden_grad = back.astype(BF)
    for t in range(4):
        part[t] = dot(x_t[4 * (1 - c) + t], hidden_grad).astype(BF)
    send(part, part_in, "halo sent", "part", partner)

    unsort = ones_where(row == target(col))

    def write_fine(a):
        flat = [dot_t(hidden_grad, down_w[4 * a + g]).astype(BF) for g in range(4)]
        for block in range(4):
            rows = jnp.concatenate([f[64 * block : 64 * block + 64] for f in flat], axis=0)
            fine_out[a, 4 * block : 4 * block + 4] = dot(unsort, rows).astype(BF).reshape(4, 64, 128)

    groups[0].start_second()
    write_fine(0)
    groups[1].start_second()
    own = [dot(x_t[4 * c + t], hidden_grad) for t in range(4)]
    wait("part")
    for t in range(4):
        sums[27 + t] = (own[t] + part_in[t].astype(F32)).astype(BF)
    groups[3].start_first()
    write_fine(1)
    groups[2].start_second()
    groups[0].start_third()
    groups[1].start_third()
    groups[3].start_second()
    groups[2].start_third()
    groups[0].gather_third()
    groups[1].gather_third()
    groups[3].start_third()
    groups[2].gather_third()
    groups[0].gather_second()
    groups[1].gather_second()
    groups[3].gather_third()
    groups[0].gather_first()
    groups[2].gather_second()
    groups[1].gather_first()
    groups[3].gather_second()
    groups[2].gather_first()
    groups[0].gather_core()
    groups[3].gather_first()
    groups[1].gather_core()
    groups[2].gather_core()
    groups[3].gather_core()
    for group in groups:
        group.finish()
    wait_all()


def deliver(fine, sums, fine_out, conv_out, down_out, sems):
    moves = [(sums.at[t : t + 9], conv_out.at[t : t + 9]) for t in range(0, CONV_TAPS, 9)]
    moves.append((fine, fine_out))
    for core in range(2):
        taps = sums.at[CONV_TAPS : CONV_TAPS + 4, 128 * core : 128 * core + 128]
        moves.append((taps, down_out.at[4 * core : 4 * core + 4]))
    copies = []
    for i, (src, dst) in enumerate(moves):
        copy = pltpu.make_async_copy(src, dst, sems.at[i])
        copy.start()
        copies.append(copy)
    for copy in copies:
        copy.wait()


def on_device(fine_field, down_weight, conv_weight, coarse_cotangent):
    vmem = pl.BlockSpec(memory_space=pltpu.VMEM)
    groups, streams = len(GROUPS), 2 * len(GROUPS)
    operands = (fine_field, down_weight, conv_weight, coarse_cotangent)
    operands = [pltpu.with_memory_space_constraint(x, pltpu.HBM) for x in operands]
    results = pl.pallas_call(
        kernel,
        out_shape=(
            jax.ShapeDtypeStruct(fine_field.shape, BF),
            jax.ShapeDtypeStruct((32, 256, 256), BF),
        ),
        in_specs=[pl.BlockSpec(memory_space=pltpu.HBM)] * 4,
        out_specs=(vmem, vmem),
        scratch_shapes=[
            pltpu.VMEM(fine_field.shape, BF),
            pltpu.VMEM(down_weight.shape, BF),
            pltpu.VMEM(conv_weight.shape, BF),
            pltpu.VMEM(coarse_cotangent.shape, BF),
            pltpu.VMEM((256, 1024), BF),
            pltpu.VMEM((8, 128, 256), BF),
            pltpu.VMEM((4, 2, 320, 128), BF),
            pltpu.VMEM((2, 3, 320, 256), BF),
            pltpu.VMEM((3, 4, 128, 256), BF),
            pltpu.VMEM((3, 320, 256), BF),
            pltpu.VMEM((2, 3, 320, 256), BF),
            pltpu.VMEM((31, 128, 256), BF),
            pltpu.VMEM((4, 128, 256), BF),
            pltpu.VMEM((4, 128, 256), BF),
            pltpu.VMEM((streams, 3, 4, 32, 256), BF),
            pltpu.VMEM((streams, 4, 32, 256), BF),
            pltpu.VMEM((streams, 3, 4, 16, 128), BF),
            pltpu.VMEM((groups, 8, 16, 128), BF),
            pltpu.VMEM((groups, 7, 16, 128), BF),
            pltpu.VMEM((864, 16, 128), BF),
            pltpu.SemaphoreType.DMA((SEMAPHORES,)),
        ],
        compiler_params=pltpu.CompilerParams(
            collective_id=0, has_side_effects=True, vmem_limit_bytes=36 * 1024 * 1024
        ),
        name="section_backward",
    )(*operands)
    hbm = pl.BlockSpec(memory_space=pltpu.HBM)
    return pl.pallas_call(
        deliver,
        out_shape=tuple(jax.ShapeDtypeStruct(x.shape, BF) for x in (fine_field, conv_weight, down_weight)),
        in_specs=[vmem] * 2,
        out_specs=(hbm, hbm, hbm),
        scratch_shapes=[pltpu.SemaphoreType.DMA((6,))],
        compiler_params=pltpu.CompilerParams(vmem_limit_bytes=1024 * 1024),
        name="deliver",
    )(*[pltpu.with_memory_space_constraint(r, pltpu.VMEM) for r in results])


def solution(mesh):
    in_specs = (P("gx", "gy", None, None), P(), P(), P("gx", "gy", None, None))
    out_specs = (P("gx", "gy", None, None), P(), P())
    return jax.shard_map(
        on_device, mesh=mesh, in_specs=in_specs, out_specs=out_specs, check_vma=False
    )
```

time: 73.2 us -> 64.7 us (0.88)
  Pallas kernels: 72.5 us -> 63.9 us
    pallas_call x1, Pallas kernels: 70.3 us -> 61.8 us  [on_device(): pl.pallas_call(kernel, out_shape=(jax.ShapeDtypeStruct(fine_field.shape,...]
where the time goes in v3:
time: 64.7 us; the launch traced here: 64.6 us
  Pallas kernels  63.9 us (99%)
    pallas_call x1, Pallas kernels, on_device(): pl.pallas_call(kernel, out_shape=(jax.ShapeDtypeStruct(fine_field.shape,...  61.8 us
    pallas_call x1, Pallas kernels, on_device(): pl.pallas_call(deliver, out_shape=tuple((jax.ShapeDtypeStruct(x.shape, BF...  2.18 us

profile of v3, /device:TPU:1, one launch (start us, length us, event | category | flops | bytes accessed | tf_op | source)
XLA Modules:
  0.0 64.6 jit_solution(11697184418559057174)
XLA Ops:
  0.6 61.8 %section_backward.1 = (bf16[2,16,64,128]{3,2,1,0:T(8,128)(2,1)S(1)}, bf16[32,256,256]{2,1,0:T(8,128)(2,1)S(1)}) custom-call(bf16[2,16,64,128]{3,2,1,0:T(8,128)(2,1)} %fine_in.1, bf16[8,128,256]{2,1,0:T(8,128)(2,1)} %down_in.1, bf16[27,256,256]{2,1,0:T(8,128)(2,1)} %conv_in.1, bf16[1,8,32,256]{3,2,1,0:T(8,128)(2,1)} %cot_in.1), custom_call_target="tpu_custom_call" | custom-call | tf_op jit(solution)/shard_map/section_backward/pallas_call | solution.py:410
  62.4 2.2 %deliver.1 = (bf16[2,16,64,128]{3,2,1,0:T(8,128)(2,1)}, bf16[27,256,256]{2,1,0:T(8,128)(2,1)}, bf16[8,128,256]{2,1,0:T(8,128)(2,1)}) custom-call(bf16[2,16,64,128]{3,2,1,0:T(8,128)(2,1)S(1)} %get-tuple-element.5.fine, bf16[32,256,256]{2,1,0:T(8,128)(2,1)S(1)} %get-tuple-element.6.sums), custom_call_target="tpu_custom_call" | custom-call | tf_op jit(solution)/shard_map/deliver/pallas_call | solution.py:447

commit v4 on v3

--- a/solution.py
+++ b/solution.py
@@ -11,9 +11,17 @@
 BF = jnp.bfloat16
 F32 = jnp.float32
 
-GROUPS = (((0, 4), (4, 4)), ((8, 4), (12, 4)), ((16, 4), (20, 4)), ((24, 3), (27, 4)))
+GROUPS = (
+    ((0, 4, True), (4, 4, False)),
+    ((8, 4, True), (12, 4, False)),
+    ((16, 4, True), (20, 4, False)),
+    ((24, 3, False), (27, 4, True)),
+)
+MOST = 4
+RELAYED = (0, 1, 2)
+RELAYED_SUMS = ()
 CONV_TAPS = 27
-SEMAPHORES = 54
+SEMAPHORES = 57
 
 
 def dot(a, b):
@@ -34,7 +42,7 @@
 
 def kernel(
     fine_in, down_in, conv_in, cot_in, fine_out, out,
-    fine, down_w, conv_w, cot, x_mat, x_t, q, hs, ht, gp, gs, sums, part, part_in, r1, y1, r2, z1, r3, measure, sems,
+    fine, down_w, conv_w, cot, x_mat, x_t, q, hs, ht, gp, gs, sums, part, part_in, r1, y0, y1, r2, z1, r3, measure, sems,
 ):
     gx, z = lax.axis_index("gx"), lax.axis_index("gy")
     px, py, c = gx // 8, (gx // 2) % 4, gx % 2
@@ -184,16 +192,18 @@
     for i, shift in ((0, after), (1, before)):
         gs[i, near, 32:288] = dot(shift, gp[near, 32:288]).astype(BF)
 
+    halves = (slice(0, 16), slice(16, 32))
+
     def row_block(f):
         return pl.ds(pl.multiple_of(32 * f, 32), 32)
 
     class Stream:
         def __init__(self, group, half):
             self.i, self.group = 2 * group + half, group
-            self.t0, self.n = GROUPS[group][half]
+            self.t0, self.n, x_first = GROUPS[group][half]
             self.tile0 = self.t0 - 8 * group
-            self.f, self.s = (px, py) if half == 0 else (py, px)
-            self.first, self.second = (on_x, on_y) if half == 0 else (on_y, on_x)
+            self.f, self.s = (px, py) if x_first else (py, px)
+            self.first, self.second = (on_x, on_y) if x_first else (on_y, on_x)
             self.row = c * 128 + 32 * self.f + 16 * (self.s % 2)
             self.lane = 128 * (self.s // 2)
 
@@ -202,19 +212,39 @@
 
         def tile(self, s):
             return pl.ds(pl.multiple_of(16 * (s % 2), 16), 16), pl.ds(pl.multiple_of(128 * (s // 2), 128), 128)
+
+        def half(self, f, h):
+            return pl.ds(pl.multiple_of(32 * (f % 4) + 16 * h, 16), 16)
 
         def out_rows(self, f):
             rows = pl.ds(pl.multiple_of(c * 128 + 32 * f, 32), 32)
             return out.at[self.t0 : self.t0 + self.n, rows]
 
         def start_first(self):
-            for k in (1, 3, 2):
-                src = sums.at[self.t0 : self.t0 + self.n, row_block((self.f + k) % 4)]
-                self.send(src, r1.at[self.i, k - 1, 0 : self.n], "first", self.first(k))
+            if self.group not in RELAYED_SUMS:
+                for k in (1, 3, 2):
+                    src = sums.at[self.t0 : self.t0 + self.n, row_block((self.f + k) % 4)]
+                    self.send(src, r1.at[self.i, k - 1, 0 : self.n], "first", self.first(k))
+                return
+            for k in (1, 3):
+                src = sums.at[self.t0 : self.t0 + self.n, self.half(self.f + 2, k // 2)]
+                self.send(src, r1.at[self.i, 1, 0 : self.n, halves[k // 2]], "first relay", self.first(k))
+            for k in (1, 3):
+                src = sums.at[self.t0 : self.t0 + self.n, self.half(self.f + k, 1 - k // 2)]
+                self.send(src, r1.at[self.i, k - 1, 0 : self.n, halves[1 - k // 2]], "first", self.first(k))
+
+        def relay_first(self):
+            for k in (1, 3):
+                h = k // 2
+                own = sums[self.t0 : self.t0 + self.n, self.half(self.f + k, h)].astype(F32)
+                both = own + r1[self.i, 1, 0 : self.n, halves[h]].astype(F32)
+                y0[self.i, h, 0 : self.n] = both.astype(BF)
+                src = y0.at[self.i, h, 0 : self.n]
+                self.send(src, r1.at[self.i, k - 1, 0 : self.n, halves[h]], "first", self.first(k))
 
         def start_second(self):
             total = sums[self.t0 : self.t0 + self.n, row_block(self.f)].astype(F32)
-            for k in range(3):
+            for k in (0, 2) if self.group in RELAYED_SUMS else (0, 1, 2):
                 total = total + r1[self.i, k, 0 : self.n].astype(F32)
             y1[self.i, 0 : self.n] = total.astype(BF)
             for k in (1, 3, 2):
@@ -238,9 +268,17 @@
 
         def gather_first(self):
             here = self.out_rows(self.f)
-            for k in (1, 3, 2):
+            for k in (1, 3) if self.group in RELAYED else (1, 3, 2):
                 self.send(here, here, ("gather first", k), self.first(k))
             self.send(here, here, "core", partner)
+
+        def relay(self, k):
+            f = (self.f + 4 - k) % 4
+            if self.group in RELAYED:
+                half = pl.ds(pl.multiple_of(c * 128 + 32 * f + 16 * (k // 2), 16), 16)
+                here = out.at[self.t0 : self.t0 + self.n, half]
+                self.send(here, here, ("gather first", 2), self.first(k))
+            self.gather_core(k)
 
         def gather_core(self, k):
             here = self.out_rows((self.f + 4 - k) % 4)
@@ -257,6 +295,11 @@
         def start_first(self):
             for stream in self.streams:
                 stream.start_first()
+
+        def relay_first(self):
+            wait(("first relay", self.i))
+            for stream in self.streams:
+                stream.relay_first()
 
         def start_second(self):
             wait(("first", self.i))
@@ -297,11 +340,16 @@
             for stream in self.streams:
                 stream.gather_first()
 
-        def gather_core(self):
-            for k in (1, 3, 2):
+        def relay(self):
+            for k in (1, 3):
                 wait((("gather first", k), self.i))
                 for stream in self.streams:
-                    stream.gather_core(k)
+                    stream.relay(k)
+
+        def gather_core(self):
+            wait((("gather first", 2), self.i))
+            for stream in self.streams:
+                stream.gather_core(2)
 
         def finish(self):
             wait(("core", self.i))
@@ -352,16 +400,16 @@
             fine_out[a, 4 * block : 4 * block + 4] = dot(unsort, rows).astype(BF).reshape(4, 64, 128)
 
     groups[0].start_second()
-    write_fine(0)
-    groups[1].start_second()
     own = [dot(x_t[4 * c + t], hidden_grad) for t in range(4)]
     wait("part")
     for t in range(4):
         sums[27 + t] = (own[t] + part_in[t].astype(F32)).astype(BF)
+    write_fine(0)
+    groups[1].start_second()
     groups[3].start_first()
     write_fine(1)
+    groups[0].start_third()
     groups[2].start_second()
-    groups[0].start_third()
     groups[1].start_third()
     groups[3].start_second()
     groups[2].start_third()
@@ -376,10 +424,14 @@
     groups[2].gather_second()
     groups[1].gather_first()
     groups[3].gather_second()
+    groups[0].relay()
     groups[2].gather_first()
+    groups[1].relay()
+    groups[3].gather_first()
     groups[0].gather_core()
-    groups[3].gather_first()
+    groups[2].relay()
     groups[1].gather_core()
+    groups[3].relay()
     groups[2].gather_core()
     groups[3].gather_core()
     for group in groups:
@@ -430,9 +482,10 @@
             pltpu.VMEM((31, 128, 256), BF),
             pltpu.VMEM((4, 128, 256), BF),
             pltpu.VMEM((4, 128, 256), BF),
-            pltpu.VMEM((streams, 3, 4, 32, 256), BF),
-            pltpu.VMEM((streams, 4, 32, 256), BF),
-            pltpu.VMEM((streams, 3, 4, 16, 128), BF),
+            pltpu.VMEM((streams, 3, MOST, 32, 256), BF),
+            pltpu.VMEM((streams, 2, MOST, 16, 256), BF),
+            pltpu.VMEM((streams, MOST, 32, 256), BF),
+            pltpu.VMEM((streams, 3, MOST, 16, 128), BF),
             pltpu.VMEM((groups, 8, 16, 128), BF),
             pltpu.VMEM((groups, 7, 16, 128), BF),
             pltpu.VMEM((864, 16, 128), BF),

time: 64.7 us -> 63.4 us (0.980)
  Pallas kernels: 63.9 us -> 62.7 us
    pallas_call x1, Pallas kernels: 61.8 us -> 60.5 us  [on_device(): pl.pallas_call(kernel, out_shape=(jax.ShapeDtypeStruct(fine_field.shape,...]
where the time goes in v4:
time: 63.4 us; the launch traced here: 63.3 us
  Pallas kernels  62.7 us (99%)
  between operations  0.64 us (1%)
    pallas_call x1, Pallas kernels, on_device(): pl.pallas_call(kernel, out_shape=(jax.ShapeDtypeStruct(fine_field.shape,...  60.5 us
    pallas_call x1, Pallas kernels, on_device(): pl.pallas_call(deliver, out_shape=tuple((jax.ShapeDtypeStruct(x.shape, BF...  2.18 us

profile of v4, /device:TPU:1, one launch (start us, length us, event | category | flops | bytes accessed | tf_op | source)
XLA Modules:
  0.0 63.3 jit_solution(4441744618919266083)
XLA Ops:
  0.6 60.5 %section_backward.1 = (bf16[2,16,64,128]{3,2,1,0:T(8,128)(2,1)S(1)}, bf16[32,256,256]{2,1,0:T(8,128)(2,1)S(1)}) custom-call(bf16[2,16,64,128]{3,2,1,0:T(8,128)(2,1)} %fine_in.1, bf16[8,128,256]{2,1,0:T(8,128)(2,1)} %down_in.1, bf16[27,256,256]{2,1,0:T(8,128)(2,1)} %conv_in.1, bf16[1,8,32,256]{3,2,1,0:T(8,128)(2,1)} %cot_in.1), custom_call_target="tpu_custom_call" | custom-call | tf_op jit(solution)/shard_map/section_backward/pallas_call | solution.py:462
  61.1 2.2 %deliver.1 = (bf16[2,16,64,128]{3,2,1,0:T(8,128)(2,1)}, bf16[27,256,256]{2,1,0:T(8,128)(2,1)}, bf16[8,128,256]{2,1,0:T(8,128)(2,1)}) custom-call(bf16[2,16,64,128]{3,2,1,0:T(8,128)(2,1)S(1)} %get-tuple-element.5.fine, bf16[32,256,256]{2,1,0:T(8,128)(2,1)S(1)} %get-tuple-element.6.sums), custom_call_target="tpu_custom_call" | custom-call | tf_op jit(solution)/shard_map/deliver/pallas_call | solution.py:500

commit v5 on v4

--- a/solution.py
+++ b/solution.py
@@ -19,9 +19,8 @@
 )
 MOST = 4
 RELAYED = (0, 1, 2)
-RELAYED_SUMS = ()
 CONV_TAPS = 27
-SEMAPHORES = 57
+SEMAPHORES = 54
 
 
 def dot(a, b):
@@ -42,7 +41,7 @@
 
 def kernel(
     fine_in, down_in, conv_in, cot_in, fine_out, out,
-    fine, down_w, conv_w, cot, x_mat, x_t, q, hs, ht, gp, gs, sums, part, part_in, r1, y0, y1, r2, z1, r3, measure, sems,
+    fine, down_w, conv_w, cot, x_mat, x_t, q, hs, ht, gp, gs, sums, part, part_in, r1, y1, r2, z1, r3, measure, sems,
 ):
     gx, z = lax.axis_index("gx"), lax.axis_index("gy")
     px, py, c = gx // 8, (gx // 2) % 4, gx % 2
@@ -151,6 +150,10 @@
     def clear(ref, index, rows, ok):
         old = ref[index + (rows,)]
         ref[index + (rows,)] = jnp.where(ok, old, jnp.zeros(old.shape, BF))
+
+    def transpose(plane):
+        for b in range(3):
+            ht[b, plane] = dot_t(eye, q[plane, c, 32 * b : 32 * b + 256]).astype(BF)
 
     acc = None
     for role, plane, a, side in ((0, mine, 1, 2), (1, 2 - c, 2 - 2 * c, 0), (2, far_plane, 2 * c, 1)):
@@ -174,16 +177,17 @@
         taps = conv_w[pl.ds(9 * a, 9)].reshape(2304, 256)
         term = dot(jnp.concatenate(pieces, axis=1), taps)
         acc = term if acc is None else acc + term
+        if side != 1:
+            transpose(plane)
     sig = jax.nn.sigmoid(acc)
     wait("cot")
     cotangent = cot[...].reshape(256, 256).astype(F32)
     gp[1, 32:288] = (cotangent * (sig * (1.0 + acc * (1.0 - sig)))).astype(BF)
 
     halo("grad", lambda rows: gp.at[1, rows], lambda side, rows: gp.at[sides[side][2], rows])
+    transpose(far_plane)
     wait("far")
-    for plane in range(4):
-        for b in range(3):
-            ht[b, plane] = dot_t(eye, q[plane, c, 32 * b : 32 * b + 256]).astype(BF)
+    transpose(3 - far_plane)
     for i, shift in ((0, after), (1, before)):
         gs[i, 1, 32:288] = dot(shift, gp[1, 32:288]).astype(BF)
 
@@ -191,8 +195,6 @@
     near = 2 - 2 * c
     for i, shift in ((0, after), (1, before)):
         gs[i, near, 32:288] = dot(shift, gp[near, 32:288]).astype(BF)
-
-    halves = (slice(0, 16), slice(16, 32))
 
     def row_block(f):
         return pl.ds(pl.multiple_of(32 * f, 32), 32)
@@ -213,38 +215,18 @@
         def tile(self, s):
             return pl.ds(pl.multiple_of(16 * (s % 2), 16), 16), pl.ds(pl.multiple_of(128 * (s // 2), 128), 128)
 
-        def half(self, f, h):
-            return pl.ds(pl.multiple_of(32 * (f % 4) + 16 * h, 16), 16)
-
         def out_rows(self, f):
             rows = pl.ds(pl.multiple_of(c * 128 + 32 * f, 32), 32)
             return out.at[self.t0 : self.t0 + self.n, rows]
 
         def start_first(self):
-            if self.group not in RELAYED_SUMS:
-                for k in (1, 3, 2):
-                    src = sums.at[self.t0 : self.t0 + self.n, row_block((self.f + k) % 4)]
-                    self.send(src, r1.at[self.i, k - 1, 0 : self.n], "first", self.first(k))
-                return
-            for k in (1, 3):
-                src = sums.at[self.t0 : self.t0 + self.n, self.half(self.f + 2, k // 2)]
-                self.send(src, r1.at[self.i, 1, 0 : self.n, halves[k // 2]], "first relay", self.first(k))
-            for k in (1, 3):
-                src = sums.at[self.t0 : self.t0 + self.n, self.half(self.f + k, 1 - k // 2)]
-                self.send(src, r1.at[self.i, k - 1, 0 : self.n, halves[1 - k // 2]], "first", self.first(k))
-
-        def relay_first(self):
-            for k in (1, 3):
-                h = k // 2
-                own = sums[self.t0 : self.t0 + self.n, self.half(self.f + k, h)].astype(F32)
-                both = own + r1[self.i, 1, 0 : self.n, halves[h]].astype(F32)
-                y0[self.i, h, 0 : self.n] = both.astype(BF)
-                src = y0.at[self.i, h, 0 : self.n]
-                self.send(src, r1.at[self.i, k - 1, 0 : self.n, halves[h]], "first", self.first(k))
+            for k in (1, 3, 2):
+                src = sums.at[self.t0 : self.t0 + self.n, row_block((self.f + k) % 4)]
+                self.send(src, r1.at[self.i, k - 1, 0 : self.n], "first", self.first(k))
 
         def start_second(self):
             total = sums[self.t0 : self.t0 + self.n, row_block(self.f)].astype(F32)
-            for k in (0, 2) if self.group in RELAYED_SUMS else (0, 1, 2):
+            for k in range(3):
                 total = total + r1[self.i, k, 0 : self.n].astype(F32)
             y1[self.i, 0 : self.n] = total.astype(BF)
             for k in (1, 3, 2):
@@ -295,11 +277,6 @@
         def start_first(self):
             for stream in self.streams:
                 stream.start_first()
-
-        def relay_first(self):
-            wait(("first relay", self.i))
-            for stream in self.streams:
-                stream.relay_first()
 
         def start_second(self):
             wait(("first", self.i))
@@ -404,13 +381,13 @@
     wait("part")
     for t in range(4):
         sums[27 + t] = (own[t] + part_in[t].astype(F32)).astype(BF)
-    write_fine(0)
     groups[1].start_second()
     groups[3].start_first()
-    write_fine(1)
     groups[0].start_third()
     groups[2].start_second()
     groups[1].start_third()
+    write_fine(0)
+    write_fine(1)
     groups[3].start_second()
     groups[2].start_third()
     groups[0].gather_third()
@@ -483,7 +460,6 @@
             pltpu.VMEM((4, 128, 256), BF),
             pltpu.VMEM((4, 128, 256), BF),
             pltpu.VMEM((streams, 3, MOST, 32, 256), BF),
-            pltpu.VMEM((streams, 2, MOST, 16, 256), BF),
             pltpu.VMEM((streams, MOST, 32, 256), BF),
             pltpu.VMEM((streams, 3, MOST, 16, 128), BF),
             pltpu.VMEM((groups, 8, 16, 128), BF),

time: 63.4 us -> 62.9 us (level)
  no operation moved by 1% of the time
where the time goes in v5:
time: 62.9 us; the launch traced here: 62.8 us
  Pallas kernels  62.2 us (99%)
  between operations  0.64 us (1%)
    pallas_call x1, Pallas kernels, on_device(): pl.pallas_call(kernel, out_shape=(jax.ShapeDtypeStruct(fine_field.shape,...  60 us
    pallas_call x1, Pallas kernels, on_device(): pl.pallas_call(deliver, out_shape=tuple((jax.ShapeDtypeStruct(x.shape, BF...  2.18 us

profile of v5, /device:TPU:1, one launch (start us, length us, event | category | flops | bytes accessed | tf_op | source)
XLA Modules:
  0.0 62.8 jit_solution(4310049162552036169)
XLA Ops:
  0.6 60.0 %section_backward.1 = (bf16[2,16,64,128]{3,2,1,0:T(8,128)(2,1)S(1)}, bf16[32,256,256]{2,1,0:T(8,128)(2,1)S(1)}) custom-call(bf16[2,16,64,128]{3,2,1,0:T(8,128)(2,1)} %fine_in.1, bf16[8,128,256]{2,1,0:T(8,128)(2,1)} %down_in.1, bf16[27,256,256]{2,1,0:T(8,128)(2,1)} %conv_in.1, bf16[1,8,32,256]{3,2,1,0:T(8,128)(2,1)} %cot_in.1), custom_call_target="tpu_custom_call" | custom-call | tf_op jit(solution)/shard_map/section_backward/pallas_call | solution.py:439
  60.7 2.2 %deliver.1 = (bf16[2,16,64,128]{3,2,1,0:T(8,128)(2,1)}, bf16[27,256,256]{2,1,0:T(8,128)(2,1)}, bf16[8,128,256]{2,1,0:T(8,128)(2,1)}) custom-call(bf16[2,16,64,128]{3,2,1,0:T(8,128)(2,1)S(1)} %get-tuple-element.5.fine, bf16[32,256,256]{2,1,0:T(8,128)(2,1)S(1)} %get-tuple-element.6.sums), custom_call_target="tpu_custom_call" | custom-call | tf_op jit(solution)/shard_map/deliver/pallas_call | solution.py:476

commit v6 on v5

--- a/solution.py
+++ b/solution.py
@@ -342,8 +342,8 @@
         a, b, s = t // 9, (t // 3) % 3, t % 3
         lhs = jnp.concatenate([ht[b, a], ht[b, a + 1]], axis=1)
         sums[t] = dot(lhs, both_planes[s]).astype(BF)
-        if t % 8 == 7:
-            groups[t // 8].start_first()
+        if t < 24 and t % 4 == 3:
+            groups[t // 8].streams[t // 4 % 2].start_first()
 
     for name in (("grad", 2, False), ("grad", 0, False), ("grad", 1, False), ("grad", 1, True)):
         wait(name)

time: 62.9 us -> 63.5 us (level)
  no operation moved by 1% of the time
where the time goes in v6:
time: 63.5 us; the launch traced here: 63.4 us
  Pallas kernels  62.8 us (99%)
  between operations  0.64 us (1%)
    pallas_call x1, Pallas kernels, on_device(): pl.pallas_call(kernel, out_shape=(jax.ShapeDtypeStruct(fine_field.shape,...  60.6 us
    pallas_call x1, Pallas kernels, on_device(): pl.pallas_call(deliver, out_shape=tuple((jax.ShapeDtypeStruct(x.shape, BF...  2.18 us

profile of v6, /device:TPU:1, one launch (start us, length us, event | category | flops | bytes accessed | tf_op | source)
XLA Modules:
  0.0 63.4 jit_solution(7725155229925554035)
XLA Ops:
  0.6 60.6 %section_backward.1 = (bf16[2,16,64,128]{3,2,1,0:T(8,128)(2,1)S(1)}, bf16[32,256,256]{2,1,0:T(8,128)(2,1)S(1)}) custom-call(bf16[2,16,64,128]{3,2,1,0:T(8,128)(2,1)} %fine_in.1, bf16[8,128,256]{2,1,0:T(8,128)(2,1)} %down_in.1, bf16[27,256,256]{2,1,0:T(8,128)(2,1)} %conv_in.1, bf16[1,8,32,256]{3,2,1,0:T(8,128)(2,1)} %cot_in.1), custom_call_target="tpu_custom_call" | custom-call | tf_op jit(solution)/shard_map/section_backward/pallas_call | solution.py:439
  61.2 2.2 %deliver.1 = (bf16[2,16,64,128]{3,2,1,0:T(8,128)(2,1)}, bf16[27,256,256]{2,1,0:T(8,128)(2,1)}, bf16[8,128,256]{2,1,0:T(8,128)(2,1)}) custom-call(bf16[2,16,64,128]{3,2,1,0:T(8,128)(2,1)S(1)} %get-tuple-element.5.fine, bf16[32,256,256]{2,1,0:T(8,128)(2,1)S(1)} %get-tuple-element.6.sums), custom_call_target="tpu_custom_call" | custom-call | tf_op jit(solution)/shard_map/deliver/pallas_call | solution.py:476
